TPU v7x, 512 devices: a whole 4x8x8 slice. The times are simulated.
512 devices in a mesh: ctx: 64 (over y_lo, x, z), exp: 8 (over y_hi, core).
Axes of the slice: x: 4, y: 8 (y_hi: 4, y_lo: 2; y = y_hi * 2 + y_lo), z: 8, core: 2. Of those that a mesh axis runs over, the one named last changes fastest.
Arguments:
- residual: bfloat16 [8192, 4096], P('ctx', 'exp'), may hold values from -6 to 6
- queries: bfloat16 [8192, 1024], P('ctx', 'exp'), may hold values from -9 to 9
- keys_values: bfloat16 [8192, 256], P('ctx'), may hold values from -9 to 9
- out_weight: bfloat16 [1024, 4096], P('exp', 'ctx'), may hold values from -0.5 to 0.5
- norm_gain: float32 [4096], replicated, may hold values from 0.25 to 1.75
- routes: int32 [8192, 8], P('ctx'), may hold values from 0 to 63, all different within a row; in each aligned block of 128 rows (0 to 127, 128 to 255, ...) at most 20 rows name the same one
- route_weights: float32 [8192, 8], P('ctx'), may hold values from 0.02 to 0.5
- gate_weight: bfloat16 [64, 4096, 1024], P('ctx', None, 'exp'), may hold values from -0.09375 to 0.09375
- up_weight: bfloat16 [64, 4096, 1024], P('ctx', None, 'exp'), may hold values from -0.09375 to 0.09375
- down_weight: bfloat16 [64, 1024, 4096], P('ctx', None, 'exp'), may hold values from -0.1875 to 0.1875
Outputs:
- layer_output: bfloat16 [8192, 4096], P('ctx', 'exp')
Inputs may be any that keep to these rules, and one draw needn't show every extreme that they name: `routes`: each row names 8 different experts. Within the rows of one index of ctx (aligned blocks of 128 positions) no expert is named by more than 20 rows, a bound that some block reaches.
All inputs are finite; a program needn't handle non-finite values.
Results may differ from a plain program's by a relative error of at most 0.0058.
Values may be sent and summed in bfloat16 or wider, within the bound.
No kernel may reach another device: no remote copies, remote signals or barrier semaphores. Data moves between devices by JAX's collectives and lax.ppermute only.
A program may use at most 128 MiB of HBM per device.

v0:
```python
import jax
import jax.numpy as jnp
from jax import lax
from jax.sharding import PartitionSpec as P

TOPK = 8


def normalize(row_block, norm_gain):
    as_float = row_block.astype(jnp.float32)
    inv_rms = lax.rsqrt(jnp.mean(as_float * as_float, axis=-1, keepdims=True) + 1e-06)
    return (as_float * inv_rms * norm_gain).astype(jnp.bfloat16)


def per_device(
    residual,
    queries,
    keys_values,
    out_weight,
    norm_gain,
    routes,
    route_weights,
    gate_weight,
    up_weight,
    down_weight,
):
    tokens_here = queries.shape[0]
    head_size = keys_values.shape[1] // 2
    heads_here = queries.shape[1] // head_size
    ctx_count = lax.axis_size("ctx")
    position = lax.axis_index("ctx") * tokens_here + jnp.arange(tokens_here, dtype=jnp.int32)
    query_heads = queries.reshape(tokens_here, heads_here, head_size)
    score_scale = head_size ** (-0.5)
    shard_piece = lax.all_gather(keys_values, "ctx", axis=0, tiled=True)
    running_max = jnp.full((tokens_here, heads_here), -1e30, jnp.float32)
    key_block = shard_piece[:, :head_size]
    value_block = shard_piece[:, head_size:].astype(jnp.float32)
    scores = (
        jnp.einsum("thd,kd->thk", query_heads, key_block, preferred_element_type=jnp.float32)
        * score_scale
    )
    key_position = jnp.arange(shard_piece.shape[0], dtype=jnp.int32)
    visible = key_position[None, None, :] <= position[:, None, None]
    scores = jnp.where(visible, scores, -1e30)
    newest = jnp.maximum(running_max, jnp.max(scores, axis=-1))
    weights = jnp.where(visible, jnp.exp(scores - newest[:, :, None]), 0.0)
    running_sum = jnp.sum(weights, axis=-1)
    summed = jnp.einsum("thk,kd->thd", weights, value_block, precision=lax.Precision.HIGHEST)
    running_max, running_sum, summed = (newest, running_sum, summed)
    attention = (
        (summed / running_sum[:, :, None])
        .reshape(tokens_here, heads_here * head_size)
        .astype(jnp.bfloat16)
    )
    head_terms = jnp.dot(
        attention,
        lax.all_gather(out_weight, "ctx", axis=1, tiled=True),
        preferred_element_type=jnp.float32,
    )
    attended = lax.psum_scatter(head_terms, "exp", scatter_dimension=1, tiled=True)
    mixed_rows = (residual.astype(jnp.float32) + attended).astype(jnp.bfloat16)
    pair_count = tokens_here * TOPK
    flat_routes = routes.reshape(pair_count)
    capacity = 5 * tokens_here * TOPK // (4 * ctx_count)
    onehot = (flat_routes[:, None] == jnp.arange(ctx_count, dtype=jnp.int32)[None, :]).astype(
        jnp.bfloat16
    )
    pair_index = jnp.arange(pair_count, dtype=jnp.int32)
    earlier = (pair_index[None, :] < pair_index[:, None]).astype(jnp.bfloat16)
    counts = jnp.dot(earlier, onehot, preferred_element_type=jnp.float32)
    slot_index = jnp.sum(counts * onehot.astype(jnp.float32), axis=1).astype(jnp.int32)
    destination = flat_routes * capacity + slot_index
    owner_token = pair_index // TOPK
    slot_token = (
        jnp.full((ctx_count * capacity,), tokens_here, jnp.int32).at[destination].set(owner_token)
    )
    full_rows = lax.all_gather(mixed_rows, "exp", axis=1, tiled=True)
    normed = normalize(full_rows, norm_gain)
    padded = jnp.concatenate([normed, jnp.zeros((1, normed.shape[1]), jnp.bfloat16)], axis=0)
    outgoing = padded[slot_token]
    arrived = lax.all_to_all(
        outgoing.reshape(ctx_count, capacity, normed.shape[1]),
        "ctx",
        split_axis=0,
        concat_axis=0,
        tiled=True,
    )
    expert_rows = arrived.reshape(ctx_count * capacity, normed.shape[1])
    hidden_width = gate_weight.shape[2]
    joined_weight = jnp.concatenate([gate_weight[0], up_weight[0]], axis=1)
    joined_value = jnp.dot(expert_rows, joined_weight, preferred_element_type=jnp.float32)
    hidden = (jax.nn.silu(joined_value[:, :hidden_width]) * joined_value[:, hidden_width:]).astype(
        jnp.bfloat16
    )
    down_rows = down_weight[0]
    expert_out = jnp.dot(
        lax.all_gather(hidden, "exp", axis=1, tiled=True),
        down_rows,
        preferred_element_type=jnp.float32,
    )
    returned = lax.all_to_all(
        expert_out.astype(jnp.bfloat16).reshape(ctx_count, capacity, down_rows.shape[1]),
        "ctx",
        split_axis=0,
        concat_axis=0,
        tiled=True,
    )
    picked = returned.reshape(ctx_count * capacity, down_rows.shape[1])[destination]
    picked = picked.reshape(tokens_here, TOPK, down_rows.shape[1]).astype(jnp.float32)
    expert_sum = jnp.sum(route_weights[:, :, None] * picked, axis=1)
    return (mixed_rows.astype(jnp.float32) + expert_sum).astype(jnp.bfloat16)


def solution(mesh):
    placed = (
        P("ctx", "exp"),
        P("ctx", "exp"),
        P("ctx", None),
        P("exp", "ctx"),
        P(),
        P("ctx", None),
        P("ctx", None),
        P("ctx", None, "exp"),
        P("ctx", None, "exp"),
        P("ctx", None, "exp"),
    )
    return jax.shard_map(
        per_device, mesh=mesh, in_specs=placed, out_specs=P("ctx", "exp"), check_vma=False
    )
```

profile of v0, /device:TPU:1, one launch (start us, length us, event | category | flops | bytes accessed | tf_op | source)
XLA Modules:
  0.0 1165.0 jit_solution(5350069126589283845)
XLA Ops:
  6.5 0.7 all-gather.5.cloned.1.call-update
  7.3 0.7 all-gather.7.cloned.1.call-update
  8.1 271.3 %all-gather.5.cloned.1.call-done = bf16[8192,256]{1,0:T(8,128)(2,1)} async-done(((bf16[128,256]{1,0:T(8,128)(2,1)}), bf16[8192,256]{1,0:T(8,128)(2,1)}) %all-gather.5.cloned.1.call-update) | async-done | bytes 4194320 | tf_op jit(solution)/shard_map/all_gather | solution.py:34
  279.3 2.7 fusion.36
  282.1 1.1 fusion.2
  283.2 3.1 fusion.22
  286.3 291.6 %all-gather.7.cloned.1.call-done = bf16[128,4096]{0,1:T(8,128)(2,1)} async-done(((bf16[128,64]{0,1:T(8,128)(2,1)}), bf16[128,4096]{0,1:T(8,128)(2,1)}) %all-gather.7.cloned.1.call-update) | async-done | bytes 1048592 | tf_op jit(solution)/shard_map/all_gather | solution.py:57
  577.9 3.0 fusion.37
  581.0 86.4 %reduce-scatter.2.cloned.1.call-done = f32[128,512]{1,0:T(8,128)} async-done(((f32[128,4096]{1,0:T(8,128)}), f32[128,512]{1,0:T(8,128)}) %reduce-scatter.2.cloned.1.call-update) | async-done | bytes 262160 | tf_op jit(solution)/shard_map/reduce_scatter | solution.py:60
  667.4 1.6 add_convert_fusion.1
  669.1 0.1 copy.14
  669.3 0.6 fusion.18
  670.2 4.3 scatter_custom_fusion
  674.5 28.0 %all-gather.9.cloned.1.call-done = bf16[128,4096]{1,0:T(8,128)(2,1)} async-done(((bf16[128,512]{1,0:T(8,128)(2,1)}), bf16[128,4096]{1,0:T(8,128)(2,1)}) %all-gather.9.cloned.1.call-update) | async-done | bytes 1048592 | tf_op jit(solution)/shard_map/all_gather | solution.py:77
  702.5 1.5 fusion.4
  704.0 1.5 fusion.6
  705.7 8.3 gather_fusion
  714.0 14.0 %reshape.96 = bf16[64,20,4096]{2,1,0:T(8,128)(2,1)} reshape(bf16[1280,4096]{1,0:T(8,128)(2,1)} %gather_fusion) | data formatting | bytes 20971520 | tf_op jit(solution)/shard_map/reshape | solution.py:82
  728.0 300.9 %all_to_all.10 = bf16[64,20,4096]{2,1,0:T(8,128)(2,1)} all-to-all(bf16[64,20,4096]{2,1,0:T(8,128)(2,1)} %reshape.96), channel_id=1, replica_groups=mesh['ctx'=64,'exp'=8] {'ctx'}, dimensions={0} | all-to-all | bytes 20971520 | tf_op jit(solution)/shard_map/all_to_all | solution.py:81
  1028.9 14.2 %reshape.97 = bf16[1280,4096]{1,0:T(8,128)(2,1)} reshape(bf16[64,20,4096]{2,1,0:T(8,128)(2,1)} %all_to_all.10) | data formatting | bytes 20971520 | tf_op jit(solution)/shard_map/reshape | solution.py:88
  1043.2 5.6 fusion.9
  1048.8 0.9 fusion.26
  1049.7 43.8 %all-gather.11.cloned.1.call-done = bf16[1280,1024]{1,0:T(8,128)(2,1)} async-done(((bf16[1280,128]{1,0:T(8,128)(2,1)}), bf16[1280,1024]{1,0:T(8,128)(2,1)}) %all-gather.11.cloned.1.call-update) | async-done | bytes 2621456 | tf_op jit(solution)/shard_map/all_gather | solution.py:97
  1093.5 3.3 convolution_convert_fusion
  1096.8 1.3 reshape.98
  1098.1 11.7 %all-to-all-start.1 = ((bf16[64,20,512]{2,1,0:T(8,128)(2,1)}), bf16[64,20,512]{2,1,0:T(8,128)(2,1)}, u32[]{:S(2)}, u32[]{:S(2)}) async-start(bf16[64,20,512]{2,1,0:T(8,128)(2,1)} %reshape.98), calls=%async_computation.2 | async-start | bytes 3145728 | tf_op jit(solution)/shard_map/all_to_all | solution.py:101
  1109.8 0.7 copy.12
  1110.5 39.4 %all-to-all-done.1 = bf16[64,20,512]{2,1,0:T(8,128)(2,1)} async-done(((bf16[64,20,512]{2,1,0:T(8,128)(2,1)}), bf16[64,20,512]{2,1,0:T(8,128)(2,1)}, u32[]{:S(2)}, u32[]{:S(2)}) %all-to-all-start.1) | async-done | bytes 1310752 | tf_op jit(solution)/shard_map/all_to_all | solution.py:101
  1150.0 2.3 reshape.99
  1152.3 4.0 gather_fusion.1
  1156.2 1.5 fusion.13
  1157.8 0.7 add_convert_fusion
  (40 shorter events, 0.7 us)
Async XLA Ops:
  6.5 1087.0 %copy-start = (bf16[1,1024,512]{2,1,0:T(8,128)(2,1)S(1)}, bf16[1,1024,512]{2,1,0:T(8,128)(2,1)}, u32[]{:S(2)}) copy-start(bf16[1,1024,512]{2,1,0:T(8,128)(2,1)} %param.19) | copy-start | bytes 3145732
  6.5 272.8 %all-gather.5.cloned.1.call-start = ((), (), s32[]{:S(2)}) async-start(), calls=%async_computation.3 | async-start | bytes 4259840 | tf_op jit(solution)/shard_map/all_gather | solution.py:34
  7.3 570.7 %all-gather.7.cloned.1.call-start = ((), (), s32[]{:S(2)}) async-start(), calls=%async_computation.4 | async-start | bytes 1064960 | tf_op jit(solution)/shard_map/all_gather | solution.py:57
  8.0 659.4 %reduce-scatter.2.cloned.1.call-start = ((), (), s32[]{:S(2)}) async-start(), calls=%async_computation.5 | async-start | bytes 2359296 | tf_op jit(solution)/shard_map/reduce_scatter | solution.py:60
  279.3 3.8 copy-start.6
  286.3 381.1 %copy-start.2 = (bf16[128,512]{1,0:T(8,128)(2,1)S(1)}, bf16[128,512]{1,0:T(8,128)(2,1)}, u32[]{:S(2)}) copy-start(bf16[128,512]{1,0:T(8,128)(2,1)} %param.10) | copy-start | bytes 393220
  286.3 382.8 %copy-start.4 = (s32[128,8]{0,1:T(8,128)S(1)}, s32[128,8]{0,1:T(8,128)}, u32[]{:S(2)}) copy-start(s32[128,8]{0,1:T(8,128)} %param.15) | copy-start | bytes 12292
  286.3 417.7 %copy-start.3 = (f32[4096]{0:T(1024)S(1)}, f32[4096]{0:T(1024)}, u32[]{:S(2)}) copy-start(f32[4096]{0:T(1024)} %param.14) | copy-start | bytes 49156
  581.0 121.5 %all-gather.9.cloned.1.call-start = ((), (), s32[]{:S(2)}) async-start(), calls=%async_computation.6 | async-start | bytes 1179648 | tf_op jit(solution)/shard_map/all_gather | solution.py:77
  669.0 424.4 %all-gather.11.cloned.1.call-start = ((), (), s32[]{:S(2)}) async-start(), calls=%async_computation.7 | async-start | bytes 2949120 | tf_op jit(solution)/shard_map/all_gather | solution.py:97
  1028.9 14.3 %copy-start.7 = (bf16[1,4096,128]{2,1,0:T(8,128)(2,1)S(1)}, bf16[1,4096,128]{2,1,0:T(8,128)(2,1)}, u32[]{:S(2)}) copy-start(bf16[1,4096,128]{2,1,0:T(8,128)(2,1)} %param.18) | copy-start | bytes 3145732
  1028.9 14.3 %copy-start.8 = (bf16[1,4096,128]{2,1,0:T(8,128)(2,1)S(1)}, bf16[1,4096,128]{2,1,0:T(8,128)(2,1)}, u32[]{:S(2)}) copy-start(bf16[1,4096,128]{2,1,0:T(8,128)(2,1)} %param.17) | copy-start | bytes 3145732
  1096.8 13.1 %copy-start.5 = (f32[128,8]{0,1:T(8,128)S(1)}, f32[128,8]{0,1:T(8,128)}, u32[]{:S(2)}) copy-start(f32[128,8]{0,1:T(8,128)} %param.16) | copy-start | bytes 12292
  1098.1 51.9 %all-to-all-start.1 = ((bf16[64,20,512]{2,1,0:T(8,128)(2,1)}), bf16[64,20,512]{2,1,0:T(8,128)(2,1)}, u32[]{:S(2)}, u32[]{:S(2)}) async-start(bf16[64,20,512]{2,1,0:T(8,128)(2,1)} %reshape.98), calls=%async_computation.2 | async-start | bytes 3145728 | tf_op jit(solution)/shard_map/all_to_all | solution.py:101
  1152.3 5.5 copy-start.1
Sparse Core Ops, SparseCore 0:
  9.4 269.8 all-gather.4
  281.4 296.4 all-gather.6
  581.1 86.2 reduce-scatter.1
  669.4 33.0 all-gather.8
  1049.8 43.5 all-gather.10
where the time goes:
time: 1170 us
  waiting for transfers between devices  762 us (65%)
  blocking collectives  301 us (26%)
  local copies, waits for them, and re-layouts  49.6 us (4%)
  matrix products  18.3 us (2%)
  between operations  13.4 us (1%)
  starting transfers between devices  11.9 us (1%)
    all_to_all x1, blocking collectives, per_device(): lax.all_to_all(outgoing.reshape(ctx_count, capacity, normed.shape[1]), 'c...  301 us
    all_gather x1, waiting for transfers between devices, per_device(): lax.all_gather(out_weight, 'ctx', axis=1, tiled=True)  292 us
    all_gather x1, waiting for transfers between devices, per_device(): shard_piece = lax.all_gather(keys_values, 'ctx', axis=0, tiled=True)  271 us
    reduce_scatter x1, waiting for transfers between devices, per_device(): lax.psum_scatter(head_terms, 'exp', scatter_dimension=1, tiled=True)  86.4 us
    all_gather x1, waiting for transfers between devices, per_device(): lax.all_gather(hidden, 'exp', axis=1, tiled=True)  43.8 us
    all_to_all x1, waiting for transfers between devices, per_device(): lax.all_to_all(expert_out.astype(jnp.bfloat16).reshape(ctx_count, capacit...  39.4 us
    all_gather x1, waiting for transfers between devices, per_device(): full_rows = lax.all_gather(mixed_rows, 'exp', axis=1, tiled=True)  28 us
  transfers between devices with their start and end apart: 6, of which 6 were waited for; matrix products, arithmetic and copies ran while one was open for 1% of the time, Pallas kernels for 0%

commit v1 on v0

v1 whole, which is shorter than its diff:
```python
import jax
import jax.numpy as jnp
import numpy as np
from jax import lax
from jax.experimental import pallas as pl
from jax.experimental.pallas import tpu as pltpu
from jax.sharding import Mesh
from jax.sharding import PartitionSpec as P

AXES = ("y_lo", "x", "z", "y_hi", "core")
CTX = ("y_lo", "x", "z")
YX = ("y_lo", "x")
EXP = ("y_hi", "core")
CAP = 20
HALF = CAP // 2
F32 = jnp.float32
BF16 = jnp.bfloat16
NEG = -1e30


def rounded(v):
    return lax.reduce_precision(v, 8, 7)


def split3(v):
    hi = rounded(v)
    mid = rounded(v - hi)
    low = v - hi - mid
    return hi.astype(BF16), mid.astype(BF16), low.astype(BF16)


def place_out_weight(columns):
    swap = [(p * 8 + e, e * 8 + p) for p in range(8) for e in range(8)]
    return lax.ppermute(columns, YX + EXP, swap)


def swap_cores(block):
    return lax.ppermute(block, "core", [(0, 1), (1, 0)])


def shift(block, step):
    return lax.ppermute(block, "y_hi", [(i, (i + step) % 4) for i in range(4)])


def own_first(block, axis):
    return jnp.where(lax.axis_index("core") == 0, block, jnp.flip(block, axis))


def near_weights(gate_weight, up_weight):
    row = lax.axis_index("y_hi")
    joined = jnp.concatenate([gate_weight, up_weight], axis=1).reshape(4, 2, 512, 256)
    joined = own_first(joined, 1).reshape(4, 1024, 256)
    return [lax.dynamic_index_in_dim(joined, (row + k) % 4, 0, keepdims=False) for k in (0, 1, 3, 2)]


def attention_rows(queries, keys_values, out_weight, down):
    tokens = queries.shape[0]
    ctx = lax.axis_index(CTX)
    part = lax.axis_index(EXP)
    rows = tokens // 8
    gathered = lax.all_gather(
        jnp.concatenate([queries, out_weight.T], axis=0), EXP, axis=0, tiled=False
    )
    all_queries = gathered[:, :tokens]
    columns = place_out_weight(gathered[:, tokens:])
    projection = lax.all_gather(columns, "z", axis=1, tiled=False)
    own = lax.dynamic_slice_in_dim(keys_values, part * rows, rows, axis=0)
    spread = jnp.broadcast_to(own[None], (64, rows, own.shape[1]))
    held = lax.all_to_all(spread, CTX, split_axis=0, concat_axis=0, tiled=True)
    keys = held[:, :, :128].reshape(64 * rows, 128)
    values = held[:, :, 128:].reshape(64 * rows, 128)
    scores = jnp.einsum("htd,kd->htk", all_queries, keys, preferred_element_type=F32) * (128**-0.5)
    key_index = jnp.arange(64 * rows, dtype=jnp.int32)
    key_position = (key_index // rows) * tokens + part * rows + key_index % rows
    position = ctx * tokens + jnp.arange(tokens, dtype=jnp.int32)
    visible = (key_position[None, :] <= position[:, None])[None]
    scores = jnp.where(visible, scores, NEG)
    top = jnp.max(scores, axis=-1)
    weights = jnp.where(visible, jnp.exp(scores - top[:, :, None]), 0.0)
    total = jnp.sum(weights, axis=-1)
    summed = jnp.einsum("htk,kd->htd", weights.astype(BF16), values, preferred_element_type=F32)
    seen = total > 0.0
    safe = jnp.where(seen, total, 1.0)
    mean = (summed / safe[:, :, None]).astype(BF16)
    level = jnp.where(seen, top + jnp.log(safe), NEG)
    hi, mid, low = split3(level)
    extra = jnp.stack([hi, mid, low] + [jnp.zeros_like(hi)] * 13, axis=1)
    sent = jnp.concatenate([mean, extra], axis=1)
    sent, down = lax.optimization_barrier((sent, down))
    down = jnp.concatenate([down, swap_cores(jnp.flip(down, 1))], axis=3).reshape(1024, 1024)
    came = lax.all_to_all(sent, EXP, split_axis=0, concat_axis=0, tiled=True)
    came_mean = came[:, :tokens].astype(F32)
    came_level = came[:, tokens : tokens + 3].astype(F32)
    came_level = came_level[:, 0] + (came_level[:, 1] + came_level[:, 2])
    share = jnp.exp(came_level - jnp.max(came_level, axis=0, keepdims=True))
    share = share / jnp.sum(share, axis=0, keepdims=True)
    mine = jnp.sum(came_mean * share[:, :, None], axis=0).astype(BF16)
    mine, down = lax.optimization_barrier((mine, down))
    attention = lax.all_gather(mine, EXP, axis=0, tiled=False)
    product = jnp.einsum("etr,ezcr->tzc", attention, projection, preferred_element_type=F32)
    return product.reshape(tokens, 512), down


def slot_tables(routes, route_weights):
    tokens = routes.shape[0]
    named = routes[:, :, None] == jnp.arange(64, dtype=jnp.int32)[None, None, :]
    member = jnp.any(named, axis=1)
    weight = jnp.sum(jnp.where(named, route_weights[:, :, None], 0.0), axis=1)
    order = jnp.arange(tokens, dtype=jnp.int32)
    earlier = (order[None, :] < order[:, None]).astype(BF16)
    rank = jnp.dot(earlier, member.astype(BF16), preferred_element_type=F32)
    slot = jnp.where(member, rank.astype(jnp.int32), -1).T
    here = lax.axis_index("core") * HALF + jnp.arange(HALF, dtype=jnp.int32)
    hit = slot[:, None, :] == here[None, :, None]
    onehot = hit.astype(BF16).reshape(64 * HALF, tokens)
    whole = jnp.where(hit, weight.T[:, None, :], 0.0).reshape(64 * HALF, tokens)
    high = rounded(whole)
    return onehot, jnp.concatenate([high, whole - high], axis=1).astype(BF16)


def kernel_call(body, outs, flops, moved, in_specs, vmem=24):
    whole = [pl.BlockSpec(shape, lambda i, n=len(shape): (0,) * n) for shape, _ in outs]
    return pl.pallas_call(
        body,
        grid=(1,),
        in_specs=in_specs,
        out_specs=whole,
        out_shape=[jax.ShapeDtypeStruct(shape, dtype) for shape, dtype in outs],
        compiler_params=pltpu.CompilerParams(vmem_limit_bytes=vmem * 1024 * 1024),
        cost_estimate=pl.CostEstimate(flops=flops, bytes_accessed=moved, transcendentals=0),
    )


def full(*shape):
    return pl.BlockSpec(shape, lambda i: (0,) * len(shape))


def page(k):
    return pl.BlockSpec((1, 1024, 256), lambda i: (k, 0, 0))


def dot(left, right):
    return jnp.dot(left, right, preferred_element_type=F32)


def receive_kernel(arrived, gain, low_weight, high_weight, scaled, squares, far_low, far_high):
    tiles = []
    for i in range(5):
        here = slice(128 * i, 128 * i + 128)
        rows = arrived[1024 * i : 1024 * i + 1024, :].astype(F32)
        rows = rows.reshape(128, 8, 128).reshape(128, 1024)
        block = (rows * gain[...]).astype(BF16)
        scaled[here, :] = block
        far_low[here, :] = dot(block, low_weight[...]).astype(BF16)
        far_high[here, :] = dot(block, high_weight[0]).astype(BF16)
        square = rows * rows
        total = square[:, :128]
        for j in range(1, 8):
            total = total + square[:, 128 * j : 128 * j + 128]
        total = jnp.sum(total.T, axis=0, keepdims=True)
        spread = total * 65537.0
        high = spread - (spread - total)
        tiles.append(jnp.concatenate([high, total - high], axis=1))
    tiles = jnp.concatenate(tiles + [jnp.zeros((11, 256), F32)], axis=0).astype(BF16)
    squares[...] = tiles
    far_low[640:656, :] = tiles


def near_kernel(
    scaled, squares, right_own, right_other, left_own, left_other, right_low, right_high, left_low, left_high
):
    for i in range(5):
        here = slice(128 * i, 128 * i + 128)
        block = scaled[here, :]
        right_low[here, :] = dot(block, right_own[...])
        right_high[here, :] = dot(block, right_other[0]).astype(BF16)
        left_low[here, :] = dot(block, left_own[...]).astype(BF16)
        left_high[here, :] = dot(block, left_other[0])
    right_low[640:656, :] = jnp.zeros((16, 256), F32)
    right_high[640:656, :] = squares[...]
    left_low[640:656, :] = squares[...]


def own_kernel(scaled, low_weight, high_weight, own):
    for i in range(5):
        here = slice(128 * i, 128 * i + 128)
        block = scaled[here, :]
        own[here, :256] = dot(block, low_weight[...])
        own[here, 256:] = dot(block, high_weight[0])


def hidden_kernel(own, squares, left_low, left_high, right_low, right_high, hidden):
    total = squares[...].astype(F32) + left_low[640:656, :].astype(F32)
    total = total + left_high[640:656, :].astype(F32) + right_low[640:656, :].astype(F32)
    total = total[:, :128] + total[:, 128:]
    for i in range(5):
        here = slice(128 * i, 128 * i + 128)
        scale = lax.rsqrt(total[i : i + 1, :] * (1.0 / 4096) + 1e-06)
        scale = jnp.broadcast_to(scale, (8, 128)).T[:, :1]
        for half, one, two in ((0, left_low, right_low), (1, left_high, right_high)):
            sums = own[here, 256 * half : 256 * half + 256]
            sums = (sums + one[here, :].astype(F32) + two[here, :].astype(F32)) * scale
            gate, up = sums[:, :128], sums[:, 128:]
            value = gate / (1.0 + jnp.exp(-gate)) * up
            hidden[half, here, :] = value.astype(BF16)


def expert_hidden(arrived, gain, pieces, swapped_near, swapped_far):
    weight = full(1024, 256)
    scaled, squares, far_low, far_high = kernel_call(
        receive_kernel,
        [((640, 1024), BF16), ((16, 256), BF16), ((656, 256), BF16), ((640, 256), BF16)],
        680_000_000,
        4_500_000,
        [full(5120, 128), full(1, 1024), weight, page(0)],
        60,
    )(arrived.reshape(5120, 128), gain[None], pieces[3], swapped_far)
    from_left = shift(far_low, 1)
    from_right = shift(far_high, -1)
    right_low, right_high, left_low, left_high = kernel_call(
        near_kernel,
        [((656, 256), F32), ((656, 256), BF16), ((656, 256), BF16), ((640, 256), F32)],
        1_400_000_000,
        5_500_000,
        [full(640, 1024), full(16, 256), weight, page(1), weight, page(2)],
    )(scaled, squares, pieces[1], swapped_near, pieces[2], swapped_near)
    came_left_high = shift(right_high, 1)
    came_right_low = shift(left_low, -1)
    came_left_low = shift((right_low + from_left.astype(F32)).astype(BF16), 1)
    came_right_high = shift((left_high + from_right.astype(F32)).astype(BF16), -1)
    own = kernel_call(
        own_kernel,
        [((640, 512), F32)],
        680_000_000,
        3_600_000,
        [full(640, 1024), weight, page(0)],
    )(scaled, pieces[0], swapped_near)[0]
    return kernel_call(
        hidden_kernel,
        [((2, 640, 128), BF16)],
        10_000_000,
        3_500_000,
        [full(640, 512), full(16, 256)] + [full(656, 256)] * 3 + [full(640, 256)],
    )(own, squares, came_left_low, came_left_high, came_right_low, came_right_high)[0]


def near_output_kernel(own, left, right, own_down, left_down, right_down, total):
    for i in range(5):
        here = slice(128 * i, 128 * i + 128)
        block = dot(own[0, here, :], own_down[:128, :]) + dot(own[1, here, :], own_down[128:, :])
        block = block + dot(left[0, here, :], left_down[:128, :])
        block = block + dot(left[1, here, :], left_down[128:, :])
        block = block + dot(right[0, here, :], right_down[:128, :])
        total[here, :] = block + dot(right[1, here, :], right_down[128:, :])


def final_kernel(total, far_low, far_high, weight, out):
    for i in range(5):
        here = slice(128 * i, 128 * i + 128)
        block = dot(far_low[here, :], weight[:128, :]) + dot(far_high[here, :], weight[128:, :])
        block = (total[here, :] + block).reshape(128, 8, 128)
        out[1024 * i : 1024 * i + 1024, :] = block.reshape(1024, 128).astype(BF16)


def expert_outputs(hidden, down):
    row = lax.axis_index("y_hi")

    def part(k):
        return lax.dynamic_slice_in_dim(down, (row + k) % 4 * 256, 256, axis=0)

    left = shift(hidden, 1)
    right = shift(hidden, -1)
    far_low = shift(left[0], 1)
    far_high = shift(right[1], -1)
    block, weight = full(2, 640, 128), full(256, 1024)
    total = kernel_call(
        near_output_kernel,
        [((640, 1024), F32)],
        1_000_000_000,
        5_000_000,
        [block, block, block, weight, weight, weight],
    )(hidden, left, right, part(0), part(3), part(1))[0]
    out = kernel_call(
        final_kernel,
        [((5120, 128), BF16)],
        340_000_000,
        5_000_000,
        [full(640, 1024), full(640, 128), full(640, 128), weight],
    )(total, far_low, far_high, part(2))[0]
    return out.reshape(64, 80, 128)


def per_device(
    residual,
    queries,
    keys_values,
    out_weight,
    norm_gain,
    routes,
    route_weights,
    gate_weight,
    up_weight,
    down_weight,
):
    tokens = queries.shape[0]
    row = lax.axis_index("y_hi")
    blocks = near_weights(gate_weight[0], up_weight[0])
    down = own_first(down_weight[0].reshape(4, 2, 128, 512), 1)
    attended, down = attention_rows(queries, keys_values, out_weight, down)
    attended, far = lax.optimization_barrier((attended, blocks[3]))
    far = shift(far, 2)
    mixed = (residual.astype(F32) + attended).astype(BF16)
    onehot, shares = slot_tables(routes, route_weights)
    chip_rows = jnp.concatenate([mixed, swap_cores(mixed)], axis=1)
    outgoing = jnp.dot(onehot, chip_rows, preferred_element_type=F32).astype(BF16)
    outgoing = outgoing.reshape(64, 80, 128)
    far, near = lax.optimization_barrier((far, (blocks[1], blocks[2])))
    pieces = [blocks[0], shift(near[1], -1), shift(near[0], 1), far]
    turned = jnp.flip(jnp.stack(pieces[:3]).reshape(3, 2, 512, 256), 1).reshape(3, 1024, 256)
    far_turned = jnp.flip(far.reshape(2, 512, 256), 0).reshape(1, 1024, 256)
    swapped = (swap_cores(turned), swap_cores(far_turned))
    arrived = lax.all_to_all(outgoing, CTX, split_axis=0, concat_axis=0, tiled=True)
    arrived, swapped = lax.optimization_barrier((arrived, swapped))
    gain = lax.dynamic_slice_in_dim(norm_gain, row * 1024, 1024)
    gain = own_first(gain.reshape(2, 512), 0).reshape(1024)
    hidden = expert_hidden(arrived, gain, pieces, *swapped)
    expert_out = expert_outputs(hidden, down)
    returned = lax.all_to_all(expert_out, CTX, split_axis=0, concat_axis=0, tiled=True)
    returned = returned.reshape(64 * HALF, 1024)
    sums = lax.dot_general(
        shares, returned, (((0,), (0,)), ((), ())), preferred_element_type=F32
    )
    sums = sums[:tokens] + sums[tokens:]
    return (mixed.astype(F32) + (sums[:, :512] + swap_cores(sums[:, 512:]))).astype(BF16)


def solution(mesh):
    fine = Mesh(mesh.devices.reshape(2, 4, 8, 4, 2), AXES)
    placed = (
        P(CTX, EXP),
        P(CTX, EXP),
        P(CTX, None),
        P(EXP, CTX),
        P(),
        P(CTX, None),
        P(CTX, None),
        P(CTX, None, EXP),
        P(CTX, None, EXP),
        P(CTX, None, EXP),
    )
    return jax.shard_map(
        per_device, mesh=fine, in_specs=placed, out_specs=P(CTX, EXP), check_vma=False
    )
```

time: 1170 us -> 328 us (0.28)
  waiting for transfers between devices: 762 us -> 118 us
  blocking collectives: 301 us -> 36.2 us
  starting transfers between devices: 11.9 us -> 112 us
  local copies, waits for them, and re-layouts: 49.6 us -> 19.3 us
  matrix products: 18.3 us -> 5.07 us
  Pallas kernels: 0 us -> 12.7 us
    all_gather x4 -> x1, waiting for transfers between devices: 635 us -> 0.01 us  [attention_rows(): projection = lax.all_gather(columns, 'z', axis=1, tiled=False)]
    all_to_all x1 -> x0, blocking collectives: 301 us -> none  [per_device(): lax.all_to_all(outgoing.reshape(ctx_count, capacity, normed.shape[1]), 'c...]
    reduce_scatter x1 -> x0, waiting for transfers between devices: 86.4 us -> none  [per_device(): lax.psum_scatter(head_terms, 'exp', scatter_dimension=1, tiled=True)]
    ppermute x0 -> x19, waiting for transfers between devices: none -> 80.3 us  [the longest x13 78.4 us: shift(): return lax.ppermute(block, 'y_hi', [(i, (i + step) % 4) for i in range(4)])]
    ppermute x0 -> x19, starting transfers between devices: none -> 66.8 us  [the longest x13 47.1 us: shift(): return lax.ppermute(block, 'y_hi', [(i, (i + step) % 4) for i in range(4)])]
    all_gather x0 -> x2, blocking collectives: none -> 36.2 us  [the longest x1 18.3 us: attention_rows(): lax.all_gather(jnp.concatenate([queries, out_weight.T], axis=0), EXP, axi...]
    all_to_all x1 -> x4, starting transfers between devices: 11.7 us -> 44.8 us  [the longest x1 15.3 us: attention_rows(): held = lax.all_to_all(spread, CTX, split_axis=0, concat_axis=0, tiled=True)]
    reshape x4 -> x3, local copies, waits for them, and re-layouts: 31.8 us -> 2.03 us  [the longest x1 1.43 us: per_device(): outgoing = outgoing.reshape(64, 80, 128)]
  transfers between devices with their start and end apart: 6 -> 24, of which waited for: 6 -> 14; matrix products, arithmetic and copies ran while one was open for 1% -> 7% of each run, Pallas kernels for 0% -> 1%
where the time goes in v1:
time: 328 us; the launch traced here: 327 us
  waiting for transfers between devices  118 us (36%)
  starting transfers between devices  112 us (34%)
  blocking collectives  36.2 us (11%)
  local copies, waits for them, and re-layouts  19.3 us (6%)
  between operations  14.2 us (4%)
  Pallas kernels  12.7 us (4%)
  other arithmetic  9.79 us (3%)
  matrix products  5.07 us (2%)
    ppermute x13, waiting for transfers between devices, shift(): return lax.ppermute(block, 'y_hi', [(i, (i + step) % 4) for i in range(4)])  78.4 us
    ppermute x13, starting transfers between devices, shift(): return lax.ppermute(block, 'y_hi', [(i, (i + step) % 4) for i in range(4)])  47.1 us
    all_to_all x1, waiting for transfers between devices, per_device(): lax.all_to_all(expert_out, CTX, split_axis=0, concat_axis=0, tiled=True)  34 us
    all_gather x1, blocking collectives, attention_rows(): lax.all_gather(jnp.concatenate([queries, out_weight.T], axis=0), EXP, axi...  18.3 us
    all_gather x1, blocking collectives, attention_rows(): attention = lax.all_gather(mine, EXP, axis=0, tiled=False)  17.9 us
    ppermute x5, starting transfers between devices, swap_cores(): return lax.ppermute(block, 'core', [(0, 1), (1, 0)])  16.6 us
    all_to_all x1, starting transfers between devices, attention_rows(): held = lax.all_to_all(spread, CTX, split_axis=0, concat_axis=0, tiled=True)  15.3 us
    all_to_all x1, starting transfers between devices, per_device(): lax.all_to_all(expert_out, CTX, split_axis=0, concat_axis=0, tiled=True)  11.7 us
  transfers between devices with their start and end apart: 24, of which 14 were waited for; matrix products, arithmetic and copies ran while one was open for 7% of the time, Pallas kernels for 1%

profile of v1, /device:TPU:1, one launch (start us, length us, event | category | flops | bytes accessed | tf_op | source)
XLA Modules:
  0.0 327.0 jit_solution(18053814595255999296)
XLA Ops:
  8.2 15.3 %all-to-all-start = ((bf16[64,16,256]{2,1,0:T(8,128)(2,1)}), bf16[64,16,256]{2,1,0:T(8,128)(2,1)S(1)}, u32[]{:S(2)}, u32[]{:S(2)}) async-start(bf16[64,16,256]{2,1,0:T(8,128)(2,1)} %broadcast_in_dim.80), calls=%async_computation | async-start | bytes 1048576 | tf_op jit(solution)/shard_map/all_to_all | solution.py:69
  24.4 18.3 %all-gather = bf16[1536,128]{1,0:T(8,128)(2,1)S(1)} all-gather(bf16[192,128]{1,0:T(8,128)(2,1)S(1)} %pad_maximum_fusion.3), channel_id=2, replica_groups=mesh['y_lo'=2,'x'=4,'z'=8,'y_hi'=4,'core'=2] {'y_hi','core'}, dimensions={0}, use_global_device_ids=true | all-gather | bytes 442368 | tf_op jit(solution)/shard_map/all_gather | solution.py:61
  42.7 3.1 collective-permute-start.1
  55.8 10.0 %all-to-all-start.1 = ((bf16[8,144,128]{2,1,0:T(8,128)(2,1)}), bf16[8,144,128]{2,1,0:T(8,128)(2,1)S(1)}, u32[]{:S(2)}, u32[]{:S(2)}) async-start(bf16[8,144,128]{2,1,0:T(8,128)(2,1)} %concatenate.34), calls=%async_computation.1 | async-start | bytes 589824 | tf_op jit(solution)/shard_map/all_to_all | solution.py:91
  69.5 2.7 constant_dynamic-slice_fusion.4
  72.2 3.7 %all-to-all-done.1 = bf16[8,144,128]{2,1,0:T(8,128)(2,1)S(1)} async-done(((bf16[8,144,128]{2,1,0:T(8,128)(2,1)}), bf16[8,144,128]{2,1,0:T(8,128)(2,1)S(1)}, u32[]{:S(2)}, u32[]{:S(2)}) %all-to-all-start.1) | async-done | bytes 294944 | tf_op jit(solution)/shard_map/all_to_all | solution.py:91
  76.2 2.8 pad_maximum_fusion
  79.1 17.9 %all-gather.1 = bf16[1024,128]{1,0:T(8,128)(2,1)S(1)} all-gather(bf16[128,128]{1,0:T(8,128)(2,1)S(1)} %multiply_reduce_fusion), channel_id=3, replica_groups=mesh['y_lo'=2,'x'=4,'z'=8,'y_hi'=4,'core'=2] {'y_hi','core'}, dimensions={0}, use_global_device_ids=true | all-gather | bytes 294912 | tf_op jit(solution)/shard_map/all_gather | solution.py:99
  98.7 4.0 %collective-permute-start.3 = (bf16[1024,256]{1,0:T(8,128)(2,1)}, bf16[1024,256]{1,0:T(8,128)(2,1)S(1)}, u32[]{:S(2)}, u32[]{:S(2)}) collective-permute-start(bf16[1024,256]{1,0:T(8,128)(2,1)} %get-tuple-element.29), channel_id=1, source_target_pairs={{0,4},{2,6},{4,0},{6,2},{1,5},{3,7},{5,1},{7,3},{8,12},{10,14},{12... | collective-permute-start | bytes 1572872 | tf_op jit(solution)/shard_map/ppermute | solution.py:42
  102.8 5.7 %collective-permute-start.2 = (bf16[128,512]{1,0:T(8,128)(2,1)S(1)}, bf16[128,512]{1,0:T(8,128)(2,1)S(1)}, u32[]{:S(2)}, u32[]{:S(2)}) collective-permute-start(bf16[128,512]{1,0:T(8,128)(2,1)S(1)} %add_convert_fusion.2), channel_id=1, source_target_pairs={{0,1},{1,0},{2,3},{3,2},{4,5},{5,4},{6,7},{7,6},{8,9},{9,8},{10,11... | collective-permute-start | bytes 393224 | tf_op jit(solution)/shard_map/ppermute | solution.py:38
  111.5 7.7 %all-to-all-start.2 = ((bf16[64,80,128]{2,1,0:T(8,128)(2,1)}), bf16[64,80,128]{2,1,0:T(8,128)(2,1)}, u32[]{:S(2)}, u32[]{:S(2)}) async-start(bf16[64,80,128]{2,1,0:T(8,128)(2,1)} %reshape.231), calls=%async_computation.2 | async-start | bytes 2621440 | tf_op jit(solution)/shard_map/all_to_all | solution.py:322
  119.2 10.5 %collective-permute-done.3.low_weight = bf16[1024,256]{1,0:T(8,128)(2,1)S(1)} collective-permute-done((bf16[1024,256]{1,0:T(8,128)(2,1)}, bf16[1024,256]{1,0:T(8,128)(2,1)S(1)}, u32[]{:S(2)}, u32[]{:S(2)}) %collective-permute-start.3) | collective-permute-done | bytes 524320 | tf_op jit(solution)/shard_map/ppermute | solution.py:42
  132.4 4.3 %collective-permute-start.5 = (bf16[1024,256]{1,0:T(8,128)(2,1)S(1)}, bf16[1024,256]{1,0:T(8,128)(2,1)S(1)}, u32[]{:S(2)}, u32[]{:S(2)}) collective-permute-start(bf16[1024,256]{1,0:T(8,128)(2,1)S(1)} %copy-done.13), channel_id=1, source_target_pairs={{0,2},{2,4},{4,6},{6,0},{1,3},{3,5},{5,7},{7,1},{8,10},{10,12},{12... | collective-permute-start | bytes 1572872 | tf_op jit(solution)/shard_map/ppermute | solution.py:42
  136.6 9.3 %collective-permute-done.4.right_own = bf16[1024,256]{1,0:T(8,128)(2,1)S(1)} collective-permute-done((bf16[1024,256]{1,0:T(8,128)(2,1)S(1)}, bf16[1024,256]{1,0:T(8,128)(2,1)S(1)}, u32[]{:S(2)}, u32[]{:S(2)}) %collective-permute-start.4) | collective-permute-done | bytes 524320 | tf_op jit(solution)/shard_map/ppermute | solution.py:42
  145.9 21.6 %collective-permute-done.5.left_own = bf16[1024,256]{1,0:T(8,128)(2,1)S(1)} collective-permute-done((bf16[1024,256]{1,0:T(8,128)(2,1)S(1)}, bf16[1024,256]{1,0:T(8,128)(2,1)S(1)}, u32[]{:S(2)}, u32[]{:S(2)}) %collective-permute-start.5) | collective-permute-done | bytes 524320 | tf_op jit(solution)/shard_map/ppermute | solution.py:42
  169.0 2.4 collective-permute-start.6
  173.2 2.1 collective-permute-start.7
  177.4 5.3 %shard_map.100 = (bf16[640,1024]{1,0:T(8,128)(2,1)}, bf16[16,256]{1,0:T(8,128)(2,1)}, bf16[656,256]{1,0:T(8,128)(2,1)}, bf16[640,256]{1,0:T(8,128)(2,1)}) custom-call(bf16[5120,128]{1,0:T(8,128)(2,1)} %bitcast.31.arrived, f32[1,1024]{1,0:T(1,128)} %bitcast.98, bf16[1024,256]{1,0:T(8,128)(2,1)} %copy-done.12, ...), custom_call_target="tpu_custom_call" | custom-call | flops 680000000 | bytes 4500000 | tf_op jit(solution)/shard_map/pallas_call | solution.py:210
  184.7 5.5 %collective-permute-start.12 = (bf16[640,256]{1,0:T(8,128)(2,1)}, bf16[640,256]{1,0:T(8,128)(2,1)S(1)}, u32[]{:S(2)}, u32[]{:S(2)}) collective-permute-start(bf16[640,256]{1,0:T(8,128)(2,1)} %get-tuple-element.43), channel_id=1, source_target_pairs={{0,6},{2,0},{4,2},{6,4},{1,7},{3,1},{5,3},{7,5},{8,14},{10,8},{12,... | collective-permute-start | bytes 983048 | tf_op jit(solution)/shard_map/ppermute | solution.py:42
  195.7 5.5 %collective-permute-start.11 = (bf16[656,256]{1,0:T(8,128)(2,1)S(1)}, bf16[656,256]{1,0:T(8,128)(2,1)S(1)}, u32[]{:S(2)}, u32[]{:S(2)}) collective-permute-start(bf16[656,256]{1,0:T(8,128)(2,1)S(1)} %get-tuple-element.41), channel_id=1, source_target_pairs={{0,6},{2,0},{4,2},{6,4},{1,7},{3,1},{5,3},{7,5},{8,14},{10,8},{12,... | collective-permute-start | bytes 1007624 | tf_op jit(solution)/shard_map/ppermute | solution.py:42
  205.4 5.5 %collective-permute-start.13 = (bf16[640,256]{1,0:T(8,128)(2,1)S(1)}, bf16[640,256]{1,0:T(8,128)(2,1)S(1)}, u32[]{:S(2)}, u32[]{:S(2)}) collective-permute-start(bf16[640,256]{1,0:T(8,128)(2,1)S(1)} %add_convert_fusion.1), channel_id=1, source_target_pairs={{0,6},{2,0},{4,2},{6,4},{1,7},{3,1},{5,3},{7,5},{8,14},{10,8},{12,... | collective-permute-start | bytes 983048 | tf_op jit(solution)/shard_map/ppermute | solution.py:42
  211.8 10.2 %collective-permute-done.10.left_high = bf16[656,256]{1,0:T(8,128)(2,1)S(1)} collective-permute-done((bf16[656,256]{1,0:T(8,128)(2,1)S(1)}, bf16[656,256]{1,0:T(8,128)(2,1)S(1)}, u32[]{:S(2)}, u32[]{:S(2)}) %collective-permute-start.10) | collective-permute-done | bytes 335904 | tf_op jit(solution)/shard_map/ppermute | solution.py:42
  222.0 9.7 %collective-permute-done.9.left_low = bf16[656,256]{1,0:T(8,128)(2,1)S(1)} collective-permute-done((bf16[656,256]{1,0:T(8,128)(2,1)S(1)}, bf16[656,256]{1,0:T(8,128)(2,1)S(1)}, u32[]{:S(2)}, u32[]{:S(2)}) %collective-permute-start.9) | collective-permute-done | bytes 335904 | tf_op jit(solution)/shard_map/ppermute | solution.py:42
  234.2 5.5 %collective-permute-start.15 = (bf16[2,640,128]{2,1,0:T(8,128)(2,1)S(1)}, bf16[2,640,128]{2,1,0:T(8,128)(2,1)S(1)}, u32[]{:S(2)}, u32[]{:S(2)}) collective-permute-start(bf16[2,640,128]{2,1,0:T(8,128)(2,1)S(1)} %shard_map.103.own), channel_id=1, source_target_pairs={{0,6},{2,0},{4,2},{6,4},{1,7},{3,1},{5,3},{7,5},{8,14},{10,8},{12,... | collective-permute-start | bytes 983048 | tf_op jit(solution)/shard_map/ppermute | solution.py:42
  239.7 10.9 %collective-permute-done.14.left = bf16[2,640,128]{2,1,0:T(8,128)(2,1)S(1)} collective-permute-done((bf16[2,640,128]{2,1,0:T(8,128)(2,1)S(1)}, bf16[2,640,128]{2,1,0:T(8,128)(2,1)S(1)}, u32[]{:S(2)}, u32[]{:S(2)}) %collective-permute-start.14) | collective-permute-done | bytes 327712 | tf_op jit(solution)/shard_map/ppermute | solution.py:42
  252.6 5.5 %collective-permute-start.17 = (bf16[640,128]{1,0:T(8,128)(2,1)S(1)}, bf16[640,128]{1,0:T(8,128)(2,1)S(1)}, u32[]{:S(2)}, u32[]{:S(2)}) collective-permute-start(bf16[640,128]{1,0:T(8,128)(2,1)S(1)} %slice_bitcast_fusion), channel_id=1, source_target_pairs={{0,6},{2,0},{4,2},{6,4},{1,7},{3,1},{5,3},{7,5},{8,14},{10,8},{12,... | collective-permute-start | bytes 491528 | tf_op jit(solution)/shard_map/ppermute | solution.py:42
  258.3 2.2 shard_map.104.total
  261.3 3.3 %collective-permute-done.17.far_high = bf16[640,128]{1,0:T(8,128)(2,1)S(1)} collective-permute-done((bf16[640,128]{1,0:T(8,128)(2,1)S(1)}, bf16[640,128]{1,0:T(8,128)(2,1)S(1)}, u32[]{:S(2)}, u32[]{:S(2)}) %collective-permute-start.17) | collective-permute-done | bytes 163872 | tf_op jit(solution)/shard_map/ppermute | solution.py:42
  264.6 2.1 shard_map.105
  266.7 11.7 %all-to-all-start.3 = ((bf16[64,80,128]{2,1,0:T(8,128)(2,1)}), bf16[64,80,128]{2,1,0:T(8,128)(2,1)S(1)}, u32[]{:S(2)}, u32[]{:S(2)}) async-start(bf16[64,80,128]{2,1,0:T(8,128)(2,1)} %bitcast.35), calls=%async_computation.3 | async-start | bytes 2621440 | tf_op jit(solution)/shard_map/all_to_all | solution.py:328
  278.5 34.0 %all-to-all-done.3 = bf16[64,80,128]{2,1,0:T(8,128)(2,1)S(1)} async-done(((bf16[64,80,128]{2,1,0:T(8,128)(2,1)}), bf16[64,80,128]{2,1,0:T(8,128)(2,1)S(1)}, u32[]{:S(2)}, u32[]{:S(2)}) %all-to-all-start.3) | async-done | bytes 1310752 | tf_op jit(solution)/shard_map/all_to_all | solution.py:328
  313.9 4.5 %collective-permute-start.18 = (f32[128,512]{1,0:T(8,128)S(1)}, f32[128,512]{1,0:T(8,128)S(1)}, u32[]{:S(2)}, u32[]{:S(2)}) collective-permute-start(f32[128,512]{1,0:T(8,128)S(1)} %slice.74), channel_id=1, source_target_pairs={{0,1},{1,0},{2,3},{3,2},{4,5},{5,4},{6,7},{7,6},{8,9},{9,8},{10,11... | collective-permute-start | bytes 786440 | tf_op jit(solution)/shard_map/ppermute | solution.py:38
  (129 shorter events, 50.0 us)
Async XLA Ops:
  6.5 39.3 %copy-start.8 = (bf16[1,4096,128]{2,1,0:T(8,128)(2,1)S(1)}, bf16[1,4096,128]{2,1,0:T(8,128)(2,1)}, u32[]{:S(2)}) copy-start(bf16[1,4096,128]{2,1,0:T(8,128)(2,1)} %param.17) | copy-start | bytes 3145732
  6.5 39.3 %copy-start.7 = (bf16[1,4096,128]{2,1,0:T(8,128)(2,1)S(1)}, bf16[1,4096,128]{2,1,0:T(8,128)(2,1)}, u32[]{:S(2)}) copy-start(bf16[1,4096,128]{2,1,0:T(8,128)(2,1)} %param.18) | copy-start | bytes 3145732
  8.2 41.8 %all-to-all-start = ((bf16[64,16,256]{2,1,0:T(8,128)(2,1)}), bf16[64,16,256]{2,1,0:T(8,128)(2,1)S(1)}, u32[]{:S(2)}, u32[]{:S(2)}) async-start(bf16[64,16,256]{2,1,0:T(8,128)(2,1)} %broadcast_in_dim.80), calls=%async_computation | async-start | bytes 1048576 | tf_op jit(solution)/shard_map/all_to_all | solution.py:69
  23.6 73.4 %all-gather.5.cloned.1.call-start = ((), (), s32[]{:S(2)}) async-start(), calls=%async_computation.4 | async-start | bytes 1179648 | tf_op jit(solution)/shard_map/all_gather | solution.py:66
  42.7 6.6 %collective-permute-start.1 = (bf16[8,64,128]{2,1,0:T(8,128)(2,1)S(1)}, bf16[8,64,128]{2,1,0:T(8,128)(2,1)S(1)}, u32[]{:S(2)}, u32[]{:S(2)}) collective-permute-start(bf16[8,64,128]{2,1,0:T(8,128)(2,1)S(1)} %slice.68), channel_id=1, source_target_pairs={{0,0},{1,64},{2,128},{3,192},{4,256},{5,320},{6,384},{7,448},{64,1... | collective-permute-start | bytes 393224 | tf_op jit(solution)/shard_map/ppermute | solution.py:34
  55.8 20.1 %all-to-all-start.1 = ((bf16[8,144,128]{2,1,0:T(8,128)(2,1)}), bf16[8,144,128]{2,1,0:T(8,128)(2,1)S(1)}, u32[]{:S(2)}, u32[]{:S(2)}) async-start(bf16[8,144,128]{2,1,0:T(8,128)(2,1)} %concatenate.34), calls=%async_computation.1 | async-start | bytes 589824 | tf_op jit(solution)/shard_map/all_to_all | solution.py:91
  67.2 9.0 %collective-permute-start = (bf16[4,2,128,512]{3,2,1,0:T(8,128)(2,1)}, bf16[4,2,128,512]{3,2,1,0:T(8,128)(2,1)}, u32[]{:S(2)}, u32[]{:S(2)}) collective-permute-start(bf16[4,2,128,512]{3,2,1,0:T(8,128)(2,1)} %rev.24), channel_id=1, source_target_pairs={{0,1},{1,0},{2,3},{3,2},{4,5},{5,4},{6,7},{7,6},{8,9},{9,8},{10,11... | collective-permute-start | bytes 3145736 | tf_op jit(solution)/shard_map/ppermute | solution.py:38
  79.1 23.7 %copy-start.16 = (bf16[128,512]{1,0:T(8,128)(2,1)S(1)}, bf16[128,512]{1,0:T(8,128)(2,1)}, u32[]{:S(2)}) copy-start(bf16[128,512]{1,0:T(8,128)(2,1)} %param.10) | copy-start | bytes 393220
  98.7 31.0 %collective-permute-start.3 = (bf16[1024,256]{1,0:T(8,128)(2,1)}, bf16[1024,256]{1,0:T(8,128)(2,1)S(1)}, u32[]{:S(2)}, u32[]{:S(2)}) collective-permute-start(bf16[1024,256]{1,0:T(8,128)(2,1)} %get-tuple-element.29), channel_id=1, source_target_pairs={{0,4},{2,6},{4,0},{6,2},{1,5},{3,7},{5,1},{7,3},{8,12},{10,14},{12... | collective-permute-start | bytes 1572872 | tf_op jit(solution)/shard_map/ppermute | solution.py:42
  102.8 6.7 %collective-permute-start.2 = (bf16[128,512]{1,0:T(8,128)(2,1)S(1)}, bf16[128,512]{1,0:T(8,128)(2,1)S(1)}, u32[]{:S(2)}, u32[]{:S(2)}) collective-permute-start(bf16[128,512]{1,0:T(8,128)(2,1)S(1)} %add_convert_fusion.2), channel_id=1, source_target_pairs={{0,1},{1,0},{2,3},{3,2},{4,5},{5,4},{6,7},{7,6},{8,9},{9,8},{10,11... | collective-permute-start | bytes 393224 | tf_op jit(solution)/shard_map/ppermute | solution.py:38
  111.5 19.0 %copy-start.14 = (bf16[1024,256]{1,0:T(8,128)(2,1)S(1)}, bf16[1024,256]{1,0:T(8,128)(2,1)}, u32[]{:S(2)}) copy-start(bf16[1024,256]{1,0:T(8,128)(2,1)} %get-tuple-element.30) | copy-start | bytes 1572868
  111.5 20.9 %copy-start.13 = (bf16[1024,256]{1,0:T(8,128)(2,1)S(1)}, bf16[1024,256]{1,0:T(8,128)(2,1)}, u32[]{:S(2)}) copy-start(bf16[1024,256]{1,0:T(8,128)(2,1)} %get-tuple-element.31) | copy-start | bytes 1572868
  111.5 65.9 %all-to-all-start.2 = ((bf16[64,80,128]{2,1,0:T(8,128)(2,1)}), bf16[64,80,128]{2,1,0:T(8,128)(2,1)}, u32[]{:S(2)}, u32[]{:S(2)}) async-start(bf16[64,80,128]{2,1,0:T(8,128)(2,1)} %reshape.231), calls=%async_computation.2 | async-start | bytes 2621440 | tf_op jit(solution)/shard_map/all_to_all | solution.py:322
  130.4 15.5 %collective-permute-start.4 = (bf16[1024,256]{1,0:T(8,128)(2,1)S(1)}, bf16[1024,256]{1,0:T(8,128)(2,1)S(1)}, u32[]{:S(2)}, u32[]{:S(2)}) collective-permute-start(bf16[1024,256]{1,0:T(8,128)(2,1)S(1)} %copy-done.14), channel_id=1, source_target_pairs={{0,6},{2,0},{4,2},{6,4},{1,7},{3,1},{5,3},{7,5},{8,14},{10,8},{12,... | collective-permute-start | bytes 1572872 | tf_op jit(solution)/shard_map/ppermute | solution.py:42
  132.4 35.2 %collective-permute-start.5 = (bf16[1024,256]{1,0:T(8,128)(2,1)S(1)}, bf16[1024,256]{1,0:T(8,128)(2,1)S(1)}, u32[]{:S(2)}, u32[]{:S(2)}) collective-permute-start(bf16[1024,256]{1,0:T(8,128)(2,1)S(1)} %copy-done.13), channel_id=1, source_target_pairs={{0,2},{2,4},{4,6},{6,0},{1,3},{3,5},{5,7},{7,1},{8,10},{10,12},{12... | collective-permute-start | bytes 1572872 | tf_op jit(solution)/shard_map/ppermute | solution.py:42
  169.0 8.4 %collective-permute-start.6 = (bf16[3,1024,256]{2,1,0:T(8,128)(2,1)}, bf16[3,1024,256]{2,1,0:T(8,128)(2,1)S(1)}, u32[]{:S(2)}, u32[]{:S(2)}) collective-permute-start(bf16[3,1024,256]{2,1,0:T(8,128)(2,1)} %bitcast.81), channel_id=1, source_target_pairs={{0,1},{1,0},{2,3},{3,2},{4,5},{5,4},{6,7},{7,6},{8,9},{9,8},{10,11... | collective-permute-start | bytes 4718600 | tf_op jit(solution)/shard_map/ppermute | solution.py:38
  173.2 4.1 %collective-permute-start.7 = (bf16[1,1024,256]{2,1,0:T(8,128)(2,1)}, bf16[1,1024,256]{2,1,0:T(8,128)(2,1)}, u32[]{:S(2)}, u32[]{:S(2)}) collective-permute-start(bf16[1,1024,256]{2,1,0:T(8,128)(2,1)} %bitcast.92), channel_id=1, source_target_pairs={{0,1},{1,0},{2,3},{3,2},{4,5},{5,4},{6,7},{7,6},{8,9},{9,8},{10,11... | collective-permute-start | bytes 1572872 | tf_op jit(solution)/shard_map/ppermute | solution.py:38
  182.7 20.5 %collective-permute-start.8 = (bf16[656,256]{1,0:T(8,128)(2,1)}, bf16[656,256]{1,0:T(8,128)(2,1)S(1)}, u32[]{:S(2)}, u32[]{:S(2)}) collective-permute-start(bf16[656,256]{1,0:T(8,128)(2,1)} %get-tuple-element.39), channel_id=1, source_target_pairs={{0,2},{2,4},{4,6},{6,0},{1,3},{3,5},{5,7},{7,1},{8,10},{10,12},{12... | collective-permute-start | bytes 1007624 | tf_op jit(solution)/shard_map/ppermute | solution.py:42
  184.7 20.6 %collective-permute-start.12 = (bf16[640,256]{1,0:T(8,128)(2,1)}, bf16[640,256]{1,0:T(8,128)(2,1)S(1)}, u32[]{:S(2)}, u32[]{:S(2)}) collective-permute-start(bf16[640,256]{1,0:T(8,128)(2,1)} %get-tuple-element.43), channel_id=1, source_target_pairs={{0,6},{2,0},{4,2},{6,4},{1,7},{3,1},{5,3},{7,5},{8,14},{10,8},{12,... | collective-permute-start | bytes 983048 | tf_op jit(solution)/shard_map/ppermute | solution.py:42
  193.7 28.2 %collective-permute-start.10 = (bf16[656,256]{1,0:T(8,128)(2,1)S(1)}, bf16[656,256]{1,0:T(8,128)(2,1)S(1)}, u32[]{:S(2)}, u32[]{:S(2)}) collective-permute-start(bf16[656,256]{1,0:T(8,128)(2,1)S(1)} %get-tuple-element.40), channel_id=1, source_target_pairs={{0,2},{2,4},{4,6},{6,0},{1,3},{3,5},{5,7},{7,1},{8,10},{10,12},{12... | collective-permute-start | bytes 1007624 | tf_op jit(solution)/shard_map/ppermute | solution.py:42
  195.7 26.3 %collective-permute-start.11 = (bf16[656,256]{1,0:T(8,128)(2,1)S(1)}, bf16[656,256]{1,0:T(8,128)(2,1)S(1)}, u32[]{:S(2)}, u32[]{:S(2)}) collective-permute-start(bf16[656,256]{1,0:T(8,128)(2,1)S(1)} %get-tuple-element.41), channel_id=1, source_target_pairs={{0,6},{2,0},{4,2},{6,4},{1,7},{3,1},{5,3},{7,5},{8,14},{10,8},{12,... | collective-permute-start | bytes 1007624 | tf_op jit(solution)/shard_map/ppermute | solution.py:42
  203.3 28.4 %collective-permute-start.9 = (bf16[656,256]{1,0:T(8,128)(2,1)S(1)}, bf16[656,256]{1,0:T(8,128)(2,1)S(1)}, u32[]{:S(2)}, u32[]{:S(2)}) collective-permute-start(bf16[656,256]{1,0:T(8,128)(2,1)S(1)} %add_convert_fusion), channel_id=1, source_target_pairs={{0,2},{2,4},{4,6},{6,0},{1,3},{3,5},{5,7},{7,1},{8,10},{10,12},{12... | collective-permute-start | bytes 1007624 | tf_op jit(solution)/shard_map/ppermute | solution.py:42
  205.4 16.6 %collective-permute-start.13 = (bf16[640,256]{1,0:T(8,128)(2,1)S(1)}, bf16[640,256]{1,0:T(8,128)(2,1)S(1)}, u32[]{:S(2)}, u32[]{:S(2)}) collective-permute-start(bf16[640,256]{1,0:T(8,128)(2,1)S(1)} %add_convert_fusion.1), channel_id=1, source_target_pairs={{0,6},{2,0},{4,2},{6,4},{1,7},{3,1},{5,3},{7,5},{8,14},{10,8},{12,... | collective-permute-start | bytes 983048 | tf_op jit(solution)/shard_map/ppermute | solution.py:42
  211.8 46.3 %copy-start.3 = (bf16[4,2,128,1024]{3,2,1,0:T(8,128)(2,1)S(1)}, bf16[4,2,128,1024]{3,2,1,0:T(8,128)(2,1)}, u32[]{:S(2)}) copy-start(bf16[4,2,128,1024]{3,2,1,0:T(8,128)(2,1)} %pad_maximum_fusion) | copy-start | bytes 6291460
  232.3 18.3 %collective-permute-start.14 = (bf16[2,640,128]{2,1,0:T(8,128)(2,1)S(1)}, bf16[2,640,128]{2,1,0:T(8,128)(2,1)S(1)}, u32[]{:S(2)}, u32[]{:S(2)}) collective-permute-start(bf16[2,640,128]{2,1,0:T(8,128)(2,1)S(1)} %shard_map.103.own), channel_id=1, source_target_pairs={{0,2},{2,4},{4,6},{6,0},{1,3},{3,5},{5,7},{7,1},{8,10},{10,12},{12... | collective-permute-start | bytes 983048 | tf_op jit(solution)/shard_map/ppermute | solution.py:42
  234.2 18.3 %collective-permute-start.15 = (bf16[2,640,128]{2,1,0:T(8,128)(2,1)S(1)}, bf16[2,640,128]{2,1,0:T(8,128)(2,1)S(1)}, u32[]{:S(2)}, u32[]{:S(2)}) collective-permute-start(bf16[2,640,128]{2,1,0:T(8,128)(2,1)S(1)} %shard_map.103.own), channel_id=1, source_target_pairs={{0,6},{2,0},{4,2},{6,4},{1,7},{3,1},{5,3},{7,5},{8,14},{10,8},{12,... | collective-permute-start | bytes 983048 | tf_op jit(solution)/shard_map/ppermute | solution.py:42
  250.6 10.7 %collective-permute-start.16 = (bf16[640,128]{1,0:T(8,128)(2,1)S(1)}, bf16[640,128]{1,0:T(8,128)(2,1)S(1)}, u32[]{:S(2)}, u32[]{:S(2)}) collective-permute-start(bf16[640,128]{1,0:T(8,128)(2,1)S(1)} %slice_bitcast_fusion.1), channel_id=1, source_target_pairs={{0,2},{2,4},{4,6},{6,0},{1,3},{3,5},{5,7},{7,1},{8,10},{10,12},{12... | collective-permute-start | bytes 491528 | tf_op jit(solution)/shard_map/ppermute | solution.py:42
  252.6 12.0 %collective-permute-start.17 = (bf16[640,128]{1,0:T(8,128)(2,1)S(1)}, bf16[640,128]{1,0:T(8,128)(2,1)S(1)}, u32[]{:S(2)}, u32[]{:S(2)}) collective-permute-start(bf16[640,128]{1,0:T(8,128)(2,1)S(1)} %slice_bitcast_fusion), channel_id=1, source_target_pairs={{0,6},{2,0},{4,2},{6,4},{1,7},{3,1},{5,3},{7,5},{8,14},{10,8},{12,... | collective-permute-start | bytes 491528 | tf_op jit(solution)/shard_map/ppermute | solution.py:42
  266.7 11.7 %copy-start.10 = (pred[640,128]{1,0:T(32,128)(4,1)S(1)}, pred[640,128]{1,0:T(32,128)(4,1)}, u32[]{:S(2)}) copy-start(pred[640,128]{1,0:T(32,128)(4,1)} %copy-done.9) | copy-start | bytes 245764
  266.7 45.8 %all-to-all-start.3 = ((bf16[64,80,128]{2,1,0:T(8,128)(2,1)}), bf16[64,80,128]{2,1,0:T(8,128)(2,1)S(1)}, u32[]{:S(2)}, u32[]{:S(2)}) async-start(bf16[64,80,128]{2,1,0:T(8,128)(2,1)} %bitcast.35), calls=%async_computation.3 | async-start | bytes 2621440 | tf_op jit(solution)/shard_map/all_to_all | solution.py:328
  278.4 34.7 %copy-start.11 = (bf16[640,128]{1,0:T(8,128)(2,1)S(1)}, bf16[640,128]{1,0:T(8,128)(2,1)}, u32[]{:S(2)}) copy-start(bf16[640,128]{1,0:T(8,128)(2,1)} %get-tuple-element.45) | copy-start | bytes 491524
  313.9 5.6 %collective-permute-start.18 = (f32[128,512]{1,0:T(8,128)S(1)}, f32[128,512]{1,0:T(8,128)S(1)}, u32[]{:S(2)}, u32[]{:S(2)}) collective-permute-start(f32[128,512]{1,0:T(8,128)S(1)} %slice.74), channel_id=1, source_target_pairs={{0,1},{1,0},{2,3},{3,2},{4,5},{5,4},{6,7},{7,6},{8,9},{9,8},{10,11... | collective-permute-start | bytes 786440 | tf_op jit(solution)/shard_map/ppermute | solution.py:38
  (11 other events, 26.6 us)
Sparse Core Ops, SparseCore 0:
  50.2 42.0 all-gather.4

commit v2 on v1

--- a/solution.py
+++ b/solution.py
@@ -42,18 +42,20 @@
     return lax.ppermute(block, "y_hi", [(i, (i + step) % 4) for i in range(4)])
 
 
-def own_first(block, axis):
-    return jnp.where(lax.axis_index("core") == 0, block, jnp.flip(block, axis))
+def in_core_order(own, other, axis):
+    first = lax.axis_index("core") == 0
+    return jnp.concatenate(
+        [jnp.where(first, own, other), jnp.where(first, other, own)], axis=axis
+    )
 
 
 def near_weights(gate_weight, up_weight):
     row = lax.axis_index("y_hi")
-    joined = jnp.concatenate([gate_weight, up_weight], axis=1).reshape(4, 2, 512, 256)
-    joined = own_first(joined, 1).reshape(4, 1024, 256)
+    joined = jnp.concatenate([gate_weight, up_weight], axis=1).reshape(4, 1024, 256)
     return [lax.dynamic_index_in_dim(joined, (row + k) % 4, 0, keepdims=False) for k in (0, 1, 3, 2)]
 
 
-def attention_rows(queries, keys_values, out_weight, down):
+def attention_rows(queries, keys_values, out_weight, near):
     tokens = queries.shape[0]
     ctx = lax.axis_index(CTX)
     part = lax.axis_index(EXP)
@@ -61,9 +63,10 @@
     gathered = lax.all_gather(
         jnp.concatenate([queries, out_weight.T], axis=0), EXP, axis=0, tiled=False
     )
+    gathered, near = lax.optimization_barrier((gathered, near))
+    near = [shift(near[0], 1), shift(near[1], -1)]
     all_queries = gathered[:, :tokens]
     columns = place_out_weight(gathered[:, tokens:])
-    projection = lax.all_gather(columns, "z", axis=1, tiled=False)
     own = lax.dynamic_slice_in_dim(keys_values, part * rows, rows, axis=0)
     spread = jnp.broadcast_to(own[None], (64, rows, own.shape[1]))
     held = lax.all_to_all(spread, CTX, split_axis=0, concat_axis=0, tiled=True)
@@ -86,8 +89,8 @@
     hi, mid, low = split3(level)
     extra = jnp.stack([hi, mid, low] + [jnp.zeros_like(hi)] * 13, axis=1)
     sent = jnp.concatenate([mean, extra], axis=1)
-    sent, down = lax.optimization_barrier((sent, down))
-    down = jnp.concatenate([down, swap_cores(jnp.flip(down, 1))], axis=3).reshape(1024, 1024)
+    columns, _ = lax.optimization_barrier((columns, sent))
+    projection = lax.all_gather(columns, "z", axis=1, tiled=False)
     came = lax.all_to_all(sent, EXP, split_axis=0, concat_axis=0, tiled=True)
     came_mean = came[:, :tokens].astype(F32)
     came_level = came[:, tokens : tokens + 3].astype(F32)
@@ -95,10 +98,10 @@
     share = jnp.exp(came_level - jnp.max(came_level, axis=0, keepdims=True))
     share = share / jnp.sum(share, axis=0, keepdims=True)
     mine = jnp.sum(came_mean * share[:, :, None], axis=0).astype(BF16)
-    mine, down = lax.optimization_barrier((mine, down))
+    mine, near = lax.optimization_barrier((mine, near))
     attention = lax.all_gather(mine, EXP, axis=0, tiled=False)
     product = jnp.einsum("etr,ezcr->tzc", attention, projection, preferred_element_type=F32)
-    return product.reshape(tokens, 512), down
+    return product.reshape(tokens, 512), near
 
 
 def slot_tables(routes, route_weights):
@@ -135,10 +138,6 @@
     return pl.BlockSpec(shape, lambda i: (0,) * len(shape))
 
 
-def page(k):
-    return pl.BlockSpec((1, 1024, 256), lambda i: (k, 0, 0))
-
-
 def dot(left, right):
     return jnp.dot(left, right, preferred_element_type=F32)
 
@@ -152,7 +151,7 @@
         block = (rows * gain[...]).astype(BF16)
         scaled[here, :] = block
         far_low[here, :] = dot(block, low_weight[...]).astype(BF16)
-        far_high[here, :] = dot(block, high_weight[0]).astype(BF16)
+        far_high[here, :] = dot(block, high_weight[...]).astype(BF16)
         square = rows * rows
         total = square[:, :128]
         for j in range(1, 8):
@@ -173,9 +172,9 @@
         here = slice(128 * i, 128 * i + 128)
         block = scaled[here, :]
         right_low[here, :] = dot(block, right_own[...])
-        right_high[here, :] = dot(block, right_other[0]).astype(BF16)
+        right_high[here, :] = dot(block, right_other[...]).astype(BF16)
         left_low[here, :] = dot(block, left_own[...]).astype(BF16)
-        left_high[here, :] = dot(block, left_other[0])
+        left_high[here, :] = dot(block, left_other[...])
     right_low[640:656, :] = jnp.zeros((16, 256), F32)
     right_high[640:656, :] = squares[...]
     left_low[640:656, :] = squares[...]
@@ -186,7 +185,7 @@
         here = slice(128 * i, 128 * i + 128)
         block = scaled[here, :]
         own[here, :256] = dot(block, low_weight[...])
-        own[here, 256:] = dot(block, high_weight[0])
+        own[here, 256:] = dot(block, high_weight[...])
 
 
 def hidden_kernel(own, squares, left_low, left_high, right_low, right_high, hidden):
@@ -205,16 +204,16 @@
             hidden[half, here, :] = value.astype(BF16)
 
 
-def expert_hidden(arrived, gain, pieces, swapped_near, swapped_far):
+def expert_hidden(arrived, gain, low, high):
     weight = full(1024, 256)
     scaled, squares, far_low, far_high = kernel_call(
         receive_kernel,
         [((640, 1024), BF16), ((16, 256), BF16), ((656, 256), BF16), ((640, 256), BF16)],
         680_000_000,
         4_500_000,
-        [full(5120, 128), full(1, 1024), weight, page(0)],
+        [full(5120, 128), full(1, 1024), weight, weight],
         60,
-    )(arrived.reshape(5120, 128), gain[None], pieces[3], swapped_far)
+    )(arrived.reshape(5120, 128), gain[None], low[3], high[3])
     from_left = shift(far_low, 1)
     from_right = shift(far_high, -1)
     right_low, right_high, left_low, left_high = kernel_call(
@@ -222,8 +221,8 @@
         [((656, 256), F32), ((656, 256), BF16), ((656, 256), BF16), ((640, 256), F32)],
         1_400_000_000,
         5_500_000,
-        [full(640, 1024), full(16, 256), weight, page(1), weight, page(2)],
-    )(scaled, squares, pieces[1], swapped_near, pieces[2], swapped_near)
+        [full(640, 1024), full(16, 256), weight, weight, weight, weight],
+    )(scaled, squares, low[1], high[1], low[2], high[2])
     came_left_high = shift(right_high, 1)
     came_right_low = shift(left_low, -1)
     came_left_low = shift((right_low + from_left.astype(F32)).astype(BF16), 1)
@@ -233,8 +232,8 @@
         [((640, 512), F32)],
         680_000_000,
         3_600_000,
-        [full(640, 1024), weight, page(0)],
-    )(scaled, pieces[0], swapped_near)[0]
+        [full(640, 1024), weight, weight],
+    )(scaled, low[0], high[0])[0]
     return kernel_call(
         hidden_kernel,
         [((2, 640, 128), BF16)],
@@ -304,26 +303,26 @@
 ):
     tokens = queries.shape[0]
     row = lax.axis_index("y_hi")
+    first = lax.axis_index("core") == 0
     blocks = near_weights(gate_weight[0], up_weight[0])
-    down = own_first(down_weight[0].reshape(4, 2, 128, 512), 1)
-    attended, down = attention_rows(queries, keys_values, out_weight, down)
-    attended, far = lax.optimization_barrier((attended, blocks[3]))
-    far = shift(far, 2)
+    attended, near = attention_rows(
+        queries, keys_values, out_weight, (blocks[1], blocks[2])
+    )
     mixed = (residual.astype(F32) + attended).astype(BF16)
+    mixed, near, far = lax.optimization_barrier((mixed, near, blocks[3]))
     onehot, shares = slot_tables(routes, route_weights)
-    chip_rows = jnp.concatenate([mixed, swap_cores(mixed)], axis=1)
+    chip_rows = in_core_order(mixed, swap_cores(mixed), 1)
     outgoing = jnp.dot(onehot, chip_rows, preferred_element_type=F32).astype(BF16)
     outgoing = outgoing.reshape(64, 80, 128)
-    far, near = lax.optimization_barrier((far, (blocks[1], blocks[2])))
-    pieces = [blocks[0], shift(near[1], -1), shift(near[0], 1), far]
-    turned = jnp.flip(jnp.stack(pieces[:3]).reshape(3, 2, 512, 256), 1).reshape(3, 1024, 256)
-    far_turned = jnp.flip(far.reshape(2, 512, 256), 0).reshape(1, 1024, 256)
-    swapped = (swap_cores(turned), swap_cores(far_turned))
+    pieces = [blocks[0], near[1], near[0], shift(far, 2)]
+    swapped = swap_cores(jnp.stack(pieces))
+    first = lax.axis_index("core") == 0
+    low = [jnp.where(first, pieces[k], swapped[k]) for k in range(4)]
+    high = [jnp.where(first, swapped[k], pieces[k]) for k in range(4)]
+    down = in_core_order(down_weight[0], swap_cores(down_weight[0]), 1)
     arrived = lax.all_to_all(outgoing, CTX, split_axis=0, concat_axis=0, tiled=True)
-    arrived, swapped = lax.optimization_barrier((arrived, swapped))
     gain = lax.dynamic_slice_in_dim(norm_gain, row * 1024, 1024)
-    gain = own_first(gain.reshape(2, 512), 0).reshape(1024)
-    hidden = expert_hidden(arrived, gain, pieces, *swapped)
+    hidden = expert_hidden(arrived, gain, low, high)
     expert_out = expert_outputs(hidden, down)
     returned = lax.all_to_all(expert_out, CTX, split_axis=0, concat_axis=0, tiled=True)
     returned = returned.reshape(64 * HALF, 1024)
@@ -331,7 +330,9 @@
         shares, returned, (((0,), (0,)), ((), ())), preferred_element_type=F32
     )
     sums = sums[:tokens] + sums[tokens:]
-    return (mixed.astype(F32) + (sums[:, :512] + swap_cores(sums[:, 512:]))).astype(BF16)
+    mine = jnp.where(first, sums[:, :512], sums[:, 512:])
+    others = jnp.where(first, sums[:, 512:], sums[:, :512])
+    return (mixed.astype(F32) + (mine + swap_cores(others))).astype(BF16)
 
 
 def solution(mesh):

time: 328 us -> 318 us (0.970)
  waiting for transfers between devices: 118 us -> 105 us
  local copies, waits for them, and re-layouts: 19.3 us -> 10.7 us
  blocking collectives: 36.2 us -> 44.4 us
  other arithmetic: 9.79 us -> 15.1 us
    ppermute x13, waiting for transfers between devices: 78.4 us -> 33 us  [shift(): return lax.ppermute(block, 'y_hi', [(i, (i + step) % 4) for i in range(4)])]
    all_to_all x1, waiting for transfers between devices: 0.01 us -> 24.2 us  [per_device(): lax.all_to_all(outgoing, CTX, split_axis=0, concat_axis=0, tiled=True)]
    all_gather x1, blocking collectives: 17.9 us -> 27.5 us  [attention_rows(): attention = lax.all_gather(mine, EXP, axis=0, tiled=False)]
    all_to_all x1, starting transfers between devices: 7.7 us -> 17 us  [per_device(): lax.all_to_all(outgoing, CTX, split_axis=0, concat_axis=0, tiled=True)]
    all_to_all x1, waiting for transfers between devices: 3.74 us -> 10.3 us  [attention_rows(): came = lax.all_to_all(sent, EXP, split_axis=0, concat_axis=0, tiled=True)]
    all_to_all x1, starting transfers between devices: 11.7 us -> 6.38 us  [per_device(): lax.all_to_all(expert_out, CTX, split_axis=0, concat_axis=0, tiled=True)]
    all_to_all x1, starting transfers between devices: 10 us -> 5.13 us  [attention_rows(): came = lax.all_to_all(sent, EXP, split_axis=0, concat_axis=0, tiled=True)]
    rev x4 -> x0, local copies, waits for them, and re-layouts: 4.42 us -> none  [the longest x1 1.92 us: per_device(): far_turned = jnp.flip(far.reshape(2, 512, 256), 0).reshape(1, 1024, 256)]
  transfers between devices with their start and end apart: 24 -> 23, of which waited for: 14 -> 11; matrix products, arithmetic and copies ran while one was open for 7% -> 7% of each run, Pallas kernels for 1% -> 2%
where the time goes in v2:
time: 318 us; the launch traced here: 316 us
  starting transfers between devices  109 us (34%)
  waiting for transfers between devices  105 us (33%)
  blocking collectives  44.4 us (14%)
  other arithmetic  15.1 us (5%)
  between operations  14.2 us (4%)
  Pallas kernels  12.7 us (4%)
  local copies, waits for them, and re-layouts  10.7 us (3%)
  matrix products  5.07 us (2%)
    ppermute x13, starting transfers between devices, shift(): return lax.ppermute(block, 'y_hi', [(i, (i + step) % 4) for i in range(4)])  48.7 us
    all_to_all x1, waiting for transfers between devices, per_device(): lax.all_to_all(expert_out, CTX, split_axis=0, concat_axis=0, tiled=True)  33.7 us
    ppermute x13, waiting for transfers between devices, shift(): return lax.ppermute(block, 'y_hi', [(i, (i + step) % 4) for i in range(4)])  33 us
    all_gather x1, blocking collectives, attention_rows(): attention = lax.all_gather(mine, EXP, axis=0, tiled=False)  27.5 us
    all_to_all x1, waiting for transfers between devices, per_device(): lax.all_to_all(outgoing, CTX, split_axis=0, concat_axis=0, tiled=True)  24.2 us
    all_to_all x1, starting transfers between devices, per_device(): lax.all_to_all(outgoing, CTX, split_axis=0, concat_axis=0, tiled=True)  17 us
    all_gather x1, blocking collectives, attention_rows(): lax.all_gather(jnp.concatenate([queries, out_weight.T], axis=0), EXP, axi...  16.9 us
    all_to_all x1, starting transfers between devices, attention_rows(): held = lax.all_to_all(spread, CTX, split_axis=0, concat_axis=0, tiled=True)  15.3 us
  transfers between devices with their start and end apart: 23, of which 11 were waited for; matrix products, arithmetic and copies ran while one was open for 7% of the time, Pallas kernels for 2%

profile of v2, /device:TPU:1, one launch (start us, length us, event | category | flops | bytes accessed | tf_op | source)
XLA Modules:
  0.0 316.2 jit_solution(527956805758280424)
XLA Ops:
  8.2 15.3 %all-to-all-start = ((bf16[64,16,256]{2,1,0:T(8,128)(2,1)}), bf16[64,16,256]{2,1,0:T(8,128)(2,1)S(1)}, u32[]{:S(2)}, u32[]{:S(2)}) async-start(bf16[64,16,256]{2,1,0:T(8,128)(2,1)} %broadcast_in_dim.83), calls=%async_computation | async-start | bytes 1048576 | tf_op jit(solution)/shard_map/all_to_all | solution.py:72
  26.9 16.9 %all-gather = bf16[1536,128]{1,0:T(8,128)(2,1)S(1)} all-gather(bf16[192,128]{1,0:T(8,128)(2,1)S(1)} %pad_maximum_fusion.1), channel_id=2, replica_groups=mesh['y_lo'=2,'x'=4,'z'=8,'y_hi'=4,'core'=2] {'y_hi','core'}, dimensions={0}, use_global_device_ids=true | all-gather | bytes 442368 | tf_op jit(solution)/shard_map/all_gather | solution.py:63
  43.8 3.3 %collective-permute-start.2 = (bf16[8,64,128]{2,1,0:T(8,128)(2,1)S(1)}, bf16[8,64,128]{2,1,0:T(8,128)(2,1)S(1)}, u32[]{:S(2)}, u32[]{:S(2)}) collective-permute-start(bf16[8,64,128]{2,1,0:T(8,128)(2,1)S(1)} %slice.71), channel_id=1, source_target_pairs={{0,0},{1,64},{2,128},{3,192},{4,256},{5,320},{6,384},{7,448},{64,1... | collective-permute-start | bytes 393224 | tf_op jit(solution)/shard_map/ppermute | solution.py:34
  53.7 5.3 %collective-permute-start = (bf16[1024,256]{1,0:T(8,128)(2,1)}, bf16[1024,256]{1,0:T(8,128)(2,1)S(1)}, u32[]{:S(2)}, u32[]{:S(2)}) collective-permute-start(bf16[1024,256]{1,0:T(8,128)(2,1)} %get-tuple-element.25), channel_id=1, source_target_pairs={{0,2},{2,4},{4,6},{6,0},{1,3},{3,5},{5,7},{7,1},{8,10},{10,12},{12... | collective-permute-start | bytes 1572872 | tf_op jit(solution)/shard_map/ppermute | solution.py:42
  59.0 4.5 %collective-permute-start.1 = (bf16[1024,256]{1,0:T(8,128)(2,1)}, bf16[1024,256]{1,0:T(8,128)(2,1)S(1)}, u32[]{:S(2)}, u32[]{:S(2)}) collective-permute-start(bf16[1024,256]{1,0:T(8,128)(2,1)} %get-tuple-element.26), channel_id=1, source_target_pairs={{0,6},{2,0},{4,2},{6,4},{1,7},{3,1},{5,3},{7,5},{8,14},{10,8},{12,... | collective-permute-start | bytes 1572872 | tf_op jit(solution)/shard_map/ppermute | solution.py:42
  63.5 5.1 %all-to-all-start.1 = ((bf16[8,144,128]{2,1,0:T(8,128)(2,1)}), bf16[8,144,128]{2,1,0:T(8,128)(2,1)S(1)}, u32[]{:S(2)}, u32[]{:S(2)}) async-start(bf16[8,144,128]{2,1,0:T(8,128)(2,1)} %concatenate.36), calls=%async_computation.1 | async-start | bytes 589824 | tf_op jit(solution)/shard_map/all_to_all | solution.py:94
  69.2 10.3 %all-to-all-done.1 = bf16[8,144,128]{2,1,0:T(8,128)(2,1)S(1)} async-done(((bf16[8,144,128]{2,1,0:T(8,128)(2,1)}), bf16[8,144,128]{2,1,0:T(8,128)(2,1)S(1)}, u32[]{:S(2)}, u32[]{:S(2)}) %all-to-all-start.1) | async-done | bytes 294944 | tf_op jit(solution)/shard_map/all_to_all | solution.py:94
  79.8 27.5 %all-gather.1 = bf16[1024,128]{1,0:T(8,128)(2,1)S(1)} all-gather(bf16[128,128]{1,0:T(8,128)(2,1)S(1)} %multiply_reduce_fusion), channel_id=3, replica_groups=mesh['y_lo'=2,'x'=4,'z'=8,'y_hi'=4,'core'=2] {'y_hi','core'}, dimensions={0}, use_global_device_ids=true | all-gather | bytes 294912 | tf_op jit(solution)/shard_map/all_gather | solution.py:102
  109.2 4.0 %collective-permute-start.4 = (bf16[1024,256]{1,0:T(8,128)(2,1)S(1)}, bf16[1024,256]{1,0:T(8,128)(2,1)}, u32[]{:S(2)}, u32[]{:S(2)}) collective-permute-start(bf16[1024,256]{1,0:T(8,128)(2,1)S(1)} %copy-done.12), channel_id=1, source_target_pairs={{0,4},{2,6},{4,0},{6,2},{1,5},{3,7},{5,1},{7,3},{8,12},{10,14},{12... | collective-permute-start | bytes 1572872 | tf_op jit(solution)/shard_map/ppermute | solution.py:42
  118.9 17.0 %all-to-all-start.2 = ((bf16[64,80,128]{2,1,0:T(8,128)(2,1)}), bf16[64,80,128]{2,1,0:T(8,128)(2,1)}, u32[]{:S(2)}, u32[]{:S(2)}) async-start(bf16[64,80,128]{2,1,0:T(8,128)(2,1)} %reshape.209), calls=%async_computation.2 | async-start | bytes 2621440 | tf_op jit(solution)/shard_map/all_to_all | solution.py:323
  137.5 2.4 collective-permute-start.5
  141.2 2.5 collective-permute-done.5
  143.7 2.9 broadcast_select_fusion.2
  146.5 24.2 %all-to-all-done.2 = bf16[64,80,128]{2,1,0:T(8,128)(2,1)} async-done(((bf16[64,80,128]{2,1,0:T(8,128)(2,1)}), bf16[64,80,128]{2,1,0:T(8,128)(2,1)}, u32[]{:S(2)}, u32[]{:S(2)}) %all-to-all-start.2) | async-done | bytes 1310752 | tf_op jit(solution)/shard_map/all_to_all | solution.py:323
  170.7 5.4 %shard_map.100 = (bf16[640,1024]{1,0:T(8,128)(2,1)}, bf16[16,256]{1,0:T(8,128)(2,1)}, bf16[656,256]{1,0:T(8,128)(2,1)}, bf16[640,256]{1,0:T(8,128)(2,1)}) custom-call(bf16[5120,128]{1,0:T(8,128)(2,1)} %bitcast.22.arrived, f32[1,1024]{1,0:T(1,128)} %bitcast.106, bf16[1024,256]{1,0:T(8,128)(2,1)} %get-tuple-element.61.low_weight, ...), custom_call_target="tpu_custom_call" | custom-call | flops 680000000 | bytes 4500000 | tf_op jit(solution)/shard_map/pallas_call | solution.py:209
  176.1 2.4 collective-permute-start.10
  178.5 3.4 %collective-permute-start.14 = (bf16[1024,512]{1,0:T(8,128)(2,1)}, bf16[1024,512]{1,0:T(8,128)(2,1)}, u32[]{:S(2)}, u32[]{:S(2)}) collective-permute-start(bf16[1024,512]{1,0:T(8,128)(2,1)} %bitcast.94), channel_id=1, source_target_pairs={{0,1},{1,0},{2,3},{3,2},{4,5},{5,4},{6,7},{7,6},{8,9},{9,8},{10,11... | collective-permute-start | bytes 3145736 | tf_op jit(solution)/shard_map/ppermute | solution.py:38
  182.0 4.2 %collective-permute-start.6 = (bf16[656,256]{1,0:T(8,128)(2,1)}, bf16[656,256]{1,0:T(8,128)(2,1)S(1)}, u32[]{:S(2)}, u32[]{:S(2)}) collective-permute-start(bf16[656,256]{1,0:T(8,128)(2,1)} %get-tuple-element.38), channel_id=1, source_target_pairs={{0,2},{2,4},{4,6},{6,0},{1,3},{3,5},{5,7},{7,1},{8,10},{10,12},{12... | collective-permute-start | bytes 1007624 | tf_op jit(solution)/shard_map/ppermute | solution.py:42
  189.8 2.6 collective-permute-start.8
  192.4 4.8 %collective-permute-start.9 = (bf16[656,256]{1,0:T(8,128)(2,1)S(1)}, bf16[656,256]{1,0:T(8,128)(2,1)S(1)}, u32[]{:S(2)}, u32[]{:S(2)}) collective-permute-start(bf16[656,256]{1,0:T(8,128)(2,1)S(1)} %get-tuple-element.40), channel_id=1, source_target_pairs={{0,6},{2,0},{4,2},{6,4},{1,7},{3,1},{5,3},{7,5},{8,14},{10,8},{12,... | collective-permute-start | bytes 1007624 | tf_op jit(solution)/shard_map/ppermute | solution.py:42
  200.4 4.2 %collective-permute-start.7 = (bf16[656,256]{1,0:T(8,128)(2,1)S(1)}, bf16[656,256]{1,0:T(8,128)(2,1)S(1)}, u32[]{:S(2)}, u32[]{:S(2)}) collective-permute-start(bf16[656,256]{1,0:T(8,128)(2,1)S(1)} %add_convert_fusion), channel_id=1, source_target_pairs={{0,2},{2,4},{4,6},{6,0},{1,3},{3,5},{5,7},{7,1},{8,10},{10,12},{12... | collective-permute-start | bytes 1007624 | tf_op jit(solution)/shard_map/ppermute | solution.py:42
  206.6 5.7 %collective-permute-done.9.right_low = bf16[656,256]{1,0:T(8,128)(2,1)S(1)} collective-permute-done((bf16[656,256]{1,0:T(8,128)(2,1)S(1)}, bf16[656,256]{1,0:T(8,128)(2,1)S(1)}, u32[]{:S(2)}, u32[]{:S(2)}) %collective-permute-start.9) | collective-permute-done | bytes 335904 | tf_op jit(solution)/shard_map/ppermute | solution.py:42
  212.3 13.3 %collective-permute-done.11.right_high = bf16[640,256]{1,0:T(8,128)(2,1)S(1)} collective-permute-done((bf16[640,256]{1,0:T(8,128)(2,1)S(1)}, bf16[640,256]{1,0:T(8,128)(2,1)S(1)}, u32[]{:S(2)}, u32[]{:S(2)}) %collective-permute-start.11) | collective-permute-done | bytes 327712 | tf_op jit(solution)/shard_map/ppermute | solution.py:42
  225.6 7.5 %collective-permute-done.7.left_low = bf16[656,256]{1,0:T(8,128)(2,1)S(1)} collective-permute-done((bf16[656,256]{1,0:T(8,128)(2,1)S(1)}, bf16[656,256]{1,0:T(8,128)(2,1)S(1)}, u32[]{:S(2)}, u32[]{:S(2)}) %collective-permute-start.7) | collective-permute-done | bytes 335904 | tf_op jit(solution)/shard_map/ppermute | solution.py:42
  233.7 2.8 collective-permute-start.12
  236.4 4.6 %collective-permute-start.13 = (bf16[2,640,128]{2,1,0:T(8,128)(2,1)S(1)}, bf16[2,640,128]{2,1,0:T(8,128)(2,1)S(1)}, u32[]{:S(2)}, u32[]{:S(2)}) collective-permute-start(bf16[2,640,128]{2,1,0:T(8,128)(2,1)S(1)} %shard_map.103.own), channel_id=1, source_target_pairs={{0,6},{2,0},{4,2},{6,4},{1,7},{3,1},{5,3},{7,5},{8,14},{10,8},{12,... | collective-permute-start | bytes 983048 | tf_op jit(solution)/shard_map/ppermute | solution.py:42
  242.5 6.0 %collective-permute-done.12.left = bf16[2,640,128]{2,1,0:T(8,128)(2,1)S(1)} collective-permute-done((bf16[2,640,128]{2,1,0:T(8,128)(2,1)S(1)}, bf16[2,640,128]{2,1,0:T(8,128)(2,1)S(1)}, u32[]{:S(2)}, u32[]{:S(2)}) %collective-permute-start.12) | collective-permute-done | bytes 327712 | tf_op jit(solution)/shard_map/ppermute | solution.py:42
  248.6 2.7 collective-permute-start.15
  251.2 4.7 %collective-permute-start.16 = (bf16[640,128]{1,0:T(8,128)(2,1)S(1)}, bf16[640,128]{1,0:T(8,128)(2,1)S(1)}, u32[]{:S(2)}, u32[]{:S(2)}) collective-permute-start(bf16[640,128]{1,0:T(8,128)(2,1)S(1)} %slice_bitcast_fusion.3), channel_id=1, source_target_pairs={{0,6},{2,0},{4,2},{6,4},{1,7},{3,1},{5,3},{7,5},{8,14},{10,8},{12,... | collective-permute-start | bytes 491528 | tf_op jit(solution)/shard_map/ppermute | solution.py:42
  261.1 6.4 %all-to-all-start.3 = ((bf16[64,80,128]{2,1,0:T(8,128)(2,1)}), bf16[64,80,128]{2,1,0:T(8,128)(2,1)S(1)}, u32[]{:S(2)}, u32[]{:S(2)}) async-start(bf16[64,80,128]{2,1,0:T(8,128)(2,1)} %bitcast.35), calls=%async_computation.3 | async-start | bytes 2621440 | tf_op jit(solution)/shard_map/all_to_all | solution.py:327
  267.6 33.7 %all-to-all-done.3 = bf16[64,80,128]{2,1,0:T(8,128)(2,1)S(1)} async-done(((bf16[64,80,128]{2,1,0:T(8,128)(2,1)}), bf16[64,80,128]{2,1,0:T(8,128)(2,1)S(1)}, u32[]{:S(2)}, u32[]{:S(2)}) %all-to-all-start.3) | async-done | bytes 1310752 | tf_op jit(solution)/shard_map/all_to_all | solution.py:327
  302.6 4.8 %collective-permute-start.17 = (f32[128,512]{1,0:T(8,128)S(1)}, f32[128,512]{1,0:T(8,128)S(1)}, u32[]{:S(2)}, u32[]{:S(2)}) collective-permute-start(f32[128,512]{1,0:T(8,128)S(1)} %slice_select_fusion), channel_id=1, source_target_pairs={{0,1},{1,0},{2,3},{3,2},{4,5},{5,4},{6,7},{7,6},{8,9},{9,8},{10,11... | collective-permute-start | bytes 786440 | tf_op jit(solution)/shard_map/ppermute | solution.py:38
  (116 shorter events, 41.6 us)
Async XLA Ops:
  6.5 17.9 %copy-start.8 = (bf16[1,4096,128]{2,1,0:T(8,128)(2,1)S(1)}, bf16[1,4096,128]{2,1,0:T(8,128)(2,1)}, u32[]{:S(2)}) copy-start(bf16[1,4096,128]{2,1,0:T(8,128)(2,1)} %param.17) | copy-start | bytes 3145732
  8.2 39.0 %all-to-all-start = ((bf16[64,16,256]{2,1,0:T(8,128)(2,1)}), bf16[64,16,256]{2,1,0:T(8,128)(2,1)S(1)}, u32[]{:S(2)}, u32[]{:S(2)}) async-start(bf16[64,16,256]{2,1,0:T(8,128)(2,1)} %broadcast_in_dim.83), calls=%async_computation | async-start | bytes 1048576 | tf_op jit(solution)/shard_map/all_to_all | solution.py:72
  23.6 83.8 %all-gather.5.cloned.1.call-start = ((), (), s32[]{:S(2)}) async-start(), calls=%async_computation.4 | async-start | bytes 1179648 | tf_op jit(solution)/shard_map/all_gather | solution.py:93
  43.8 9.2 %collective-permute-start.2 = (bf16[8,64,128]{2,1,0:T(8,128)(2,1)S(1)}, bf16[8,64,128]{2,1,0:T(8,128)(2,1)S(1)}, u32[]{:S(2)}, u32[]{:S(2)}) collective-permute-start(bf16[8,64,128]{2,1,0:T(8,128)(2,1)S(1)} %slice.71), channel_id=1, source_target_pairs={{0,0},{1,64},{2,128},{3,192},{4,256},{5,320},{6,384},{7,448},{64,1... | collective-permute-start | bytes 393224 | tf_op jit(solution)/shard_map/ppermute | solution.py:34
  49.6 19.2 %copy-start.15 = (s32[128,8]{0,1:T(8,128)S(1)}, s32[128,8]{0,1:T(8,128)}, u32[]{:S(2)}) copy-start(s32[128,8]{0,1:T(8,128)} %param.15) | copy-start | bytes 12292
  49.6 19.2 %copy-start.16 = (f32[128,8]{0,1:T(8,128)S(1)}, f32[128,8]{0,1:T(8,128)}, u32[]{:S(2)}) copy-start(f32[128,8]{0,1:T(8,128)} %param.16) | copy-start | bytes 12292
  53.7 26.1 %collective-permute-start = (bf16[1024,256]{1,0:T(8,128)(2,1)}, bf16[1024,256]{1,0:T(8,128)(2,1)S(1)}, u32[]{:S(2)}, u32[]{:S(2)}) collective-permute-start(bf16[1024,256]{1,0:T(8,128)(2,1)} %get-tuple-element.25), channel_id=1, source_target_pairs={{0,2},{2,4},{4,6},{6,0},{1,3},{3,5},{5,7},{7,1},{8,10},{10,12},{12... | collective-permute-start | bytes 1572872 | tf_op jit(solution)/shard_map/ppermute | solution.py:42
  59.0 20.8 %collective-permute-start.1 = (bf16[1024,256]{1,0:T(8,128)(2,1)}, bf16[1024,256]{1,0:T(8,128)(2,1)S(1)}, u32[]{:S(2)}, u32[]{:S(2)}) collective-permute-start(bf16[1024,256]{1,0:T(8,128)(2,1)} %get-tuple-element.26), channel_id=1, source_target_pairs={{0,6},{2,0},{4,2},{6,4},{1,7},{3,1},{5,3},{7,5},{8,14},{10,8},{12,... | collective-permute-start | bytes 1572872 | tf_op jit(solution)/shard_map/ppermute | solution.py:42
  63.5 16.0 %all-to-all-start.1 = ((bf16[8,144,128]{2,1,0:T(8,128)(2,1)}), bf16[8,144,128]{2,1,0:T(8,128)(2,1)S(1)}, u32[]{:S(2)}, u32[]{:S(2)}) async-start(bf16[8,144,128]{2,1,0:T(8,128)(2,1)} %concatenate.36), calls=%async_computation.1 | async-start | bytes 589824 | tf_op jit(solution)/shard_map/all_to_all | solution.py:94
  69.0 40.2 %copy-start.14 = (bf16[128,512]{1,0:T(8,128)(2,1)S(1)}, bf16[128,512]{1,0:T(8,128)(2,1)}, u32[]{:S(2)}) copy-start(bf16[128,512]{1,0:T(8,128)(2,1)} %param.10) | copy-start | bytes 393220
  69.2 40.0 %copy-start.12 = (bf16[1024,256]{1,0:T(8,128)(2,1)S(1)}, bf16[1024,256]{1,0:T(8,128)(2,1)}, u32[]{:S(2)}) copy-start(bf16[1024,256]{1,0:T(8,128)(2,1)} %get-tuple-element.32) | copy-start | bytes 1572868
  79.8 36.7 %copy-start.4 = (bf16[1024,256]{1,0:T(8,128)(2,1)}, bf16[1024,256]{1,0:T(8,128)(2,1)S(1)}, u32[]{:S(2)}) copy-start(bf16[1024,256]{1,0:T(8,128)(2,1)S(1)} %collective-permute-done.1) | copy-start | bytes 1572868
  109.2 26.8 %collective-permute-start.4 = (bf16[1024,256]{1,0:T(8,128)(2,1)S(1)}, bf16[1024,256]{1,0:T(8,128)(2,1)}, u32[]{:S(2)}, u32[]{:S(2)}) collective-permute-start(bf16[1024,256]{1,0:T(8,128)(2,1)S(1)} %copy-done.12), channel_id=1, source_target_pairs={{0,4},{2,6},{4,0},{6,2},{1,5},{3,7},{5,1},{7,3},{8,12},{10,14},{12... | collective-permute-start | bytes 1572872 | tf_op jit(solution)/shard_map/ppermute | solution.py:42
  113.2 3.3 %collective-permute-start.3 = (bf16[128,512]{1,0:T(8,128)(2,1)S(1)}, bf16[128,512]{1,0:T(8,128)(2,1)S(1)}, u32[]{:S(2)}, u32[]{:S(2)}) collective-permute-start(bf16[128,512]{1,0:T(8,128)(2,1)S(1)} %add_convert_fusion.3), channel_id=1, source_target_pairs={{0,1},{1,0},{2,3},{3,2},{4,5},{5,4},{6,7},{7,6},{8,9},{9,8},{10,11... | collective-permute-start | bytes 393224 | tf_op jit(solution)/shard_map/ppermute | solution.py:38
  118.9 51.8 %all-to-all-start.2 = ((bf16[64,80,128]{2,1,0:T(8,128)(2,1)}), bf16[64,80,128]{2,1,0:T(8,128)(2,1)}, u32[]{:S(2)}, u32[]{:S(2)}) async-start(bf16[64,80,128]{2,1,0:T(8,128)(2,1)} %reshape.209), calls=%async_computation.2 | async-start | bytes 2621440 | tf_op jit(solution)/shard_map/all_to_all | solution.py:323
  137.5 6.2 %collective-permute-start.5 = (bf16[4,1024,256]{2,1,0:T(8,128)(2,1)S(1)}, bf16[4,1024,256]{2,1,0:T(8,128)(2,1)}, u32[]{:S(2)}, u32[]{:S(2)}) collective-permute-start(bf16[4,1024,256]{2,1,0:T(8,128)(2,1)S(1)} %pad_maximum_fusion), channel_id=1, source_target_pairs={{0,1},{1,0},{2,3},{3,2},{4,5},{5,4},{6,7},{7,6},{8,9},{9,8},{10,11... | collective-permute-start | bytes 6291464 | tf_op jit(solution)/shard_map/ppermute | solution.py:38
  176.1 21.1 %collective-permute-start.10 = (bf16[640,256]{1,0:T(8,128)(2,1)}, bf16[640,256]{1,0:T(8,128)(2,1)}, u32[]{:S(2)}, u32[]{:S(2)}) collective-permute-start(bf16[640,256]{1,0:T(8,128)(2,1)} %get-tuple-element.42), channel_id=1, source_target_pairs={{0,6},{2,0},{4,2},{6,4},{1,7},{3,1},{5,3},{7,5},{8,14},{10,8},{12,... | collective-permute-start | bytes 983048 | tf_op jit(solution)/shard_map/ppermute | solution.py:42
  178.5 62.6 %collective-permute-start.14 = (bf16[1024,512]{1,0:T(8,128)(2,1)}, bf16[1024,512]{1,0:T(8,128)(2,1)}, u32[]{:S(2)}, u32[]{:S(2)}) collective-permute-start(bf16[1024,512]{1,0:T(8,128)(2,1)} %bitcast.94), channel_id=1, source_target_pairs={{0,1},{1,0},{2,3},{3,2},{4,5},{5,4},{6,7},{7,6},{8,9},{9,8},{10,11... | collective-permute-start | bytes 3145736 | tf_op jit(solution)/shard_map/ppermute | solution.py:38
  182.0 18.3 %collective-permute-start.6 = (bf16[656,256]{1,0:T(8,128)(2,1)}, bf16[656,256]{1,0:T(8,128)(2,1)S(1)}, u32[]{:S(2)}, u32[]{:S(2)}) collective-permute-start(bf16[656,256]{1,0:T(8,128)(2,1)} %get-tuple-element.38), channel_id=1, source_target_pairs={{0,2},{2,4},{4,6},{6,0},{1,3},{3,5},{5,7},{7,1},{8,10},{10,12},{12... | collective-permute-start | bytes 1007624 | tf_op jit(solution)/shard_map/ppermute | solution.py:42
  189.8 16.8 %collective-permute-start.8 = (bf16[656,256]{1,0:T(8,128)(2,1)S(1)}, bf16[656,256]{1,0:T(8,128)(2,1)S(1)}, u32[]{:S(2)}, u32[]{:S(2)}) collective-permute-start(bf16[656,256]{1,0:T(8,128)(2,1)S(1)} %get-tuple-element.39), channel_id=1, source_target_pairs={{0,2},{2,4},{4,6},{6,0},{1,3},{3,5},{5,7},{7,1},{8,10},{10,12},{12... | collective-permute-start | bytes 1007624 | tf_op jit(solution)/shard_map/ppermute | solution.py:42
  192.4 19.9 %collective-permute-start.9 = (bf16[656,256]{1,0:T(8,128)(2,1)S(1)}, bf16[656,256]{1,0:T(8,128)(2,1)S(1)}, u32[]{:S(2)}, u32[]{:S(2)}) collective-permute-start(bf16[656,256]{1,0:T(8,128)(2,1)S(1)} %get-tuple-element.40), channel_id=1, source_target_pairs={{0,6},{2,0},{4,2},{6,4},{1,7},{3,1},{5,3},{7,5},{8,14},{10,8},{12,... | collective-permute-start | bytes 1007624 | tf_op jit(solution)/shard_map/ppermute | solution.py:42
  198.3 27.4 %collective-permute-start.11 = (bf16[640,256]{1,0:T(8,128)(2,1)S(1)}, bf16[640,256]{1,0:T(8,128)(2,1)S(1)}, u32[]{:S(2)}, u32[]{:S(2)}) collective-permute-start(bf16[640,256]{1,0:T(8,128)(2,1)S(1)} %add_convert_fusion.1), channel_id=1, source_target_pairs={{0,6},{2,0},{4,2},{6,4},{1,7},{3,1},{5,3},{7,5},{8,14},{10,8},{12,... | collective-permute-start | bytes 983048 | tf_op jit(solution)/shard_map/ppermute | solution.py:42
  200.4 32.7 %collective-permute-start.7 = (bf16[656,256]{1,0:T(8,128)(2,1)S(1)}, bf16[656,256]{1,0:T(8,128)(2,1)S(1)}, u32[]{:S(2)}, u32[]{:S(2)}) collective-permute-start(bf16[656,256]{1,0:T(8,128)(2,1)S(1)} %add_convert_fusion), channel_id=1, source_target_pairs={{0,2},{2,4},{4,6},{6,0},{1,3},{3,5},{5,7},{7,1},{8,10},{10,12},{12... | collective-permute-start | bytes 1007624 | tf_op jit(solution)/shard_map/ppermute | solution.py:42
  205.7 27.4 %copy-start.3 = (bf16[16,256]{1,0:T(8,128)(2,1)S(1)}, bf16[16,256]{1,0:T(8,128)(2,1)}, u32[]{:S(2)}) copy-start(bf16[16,256]{1,0:T(8,128)(2,1)} %get-tuple-element.36.squares) | copy-start | bytes 24580
  206.6 34.5 %copy-start.7 = (bf16[1,1024,512]{2,1,0:T(8,128)(2,1)S(1)}, bf16[1,1024,512]{2,1,0:T(8,128)(2,1)}, u32[]{:S(2)}) copy-start(bf16[1,1024,512]{2,1,0:T(8,128)(2,1)} %param.19) | copy-start | bytes 3145732
  233.7 14.8 %collective-permute-start.12 = (bf16[2,640,128]{2,1,0:T(8,128)(2,1)S(1)}, bf16[2,640,128]{2,1,0:T(8,128)(2,1)S(1)}, u32[]{:S(2)}, u32[]{:S(2)}) collective-permute-start(bf16[2,640,128]{2,1,0:T(8,128)(2,1)S(1)} %shard_map.103.own), channel_id=1, source_target_pairs={{0,2},{2,4},{4,6},{6,0},{1,3},{3,5},{5,7},{7,1},{8,10},{10,12},{12... | collective-permute-start | bytes 983048 | tf_op jit(solution)/shard_map/ppermute | solution.py:42
  236.4 14.8 %collective-permute-start.13 = (bf16[2,640,128]{2,1,0:T(8,128)(2,1)S(1)}, bf16[2,640,128]{2,1,0:T(8,128)(2,1)S(1)}, u32[]{:S(2)}, u32[]{:S(2)}) collective-permute-start(bf16[2,640,128]{2,1,0:T(8,128)(2,1)S(1)} %shard_map.103.own), channel_id=1, source_target_pairs={{0,6},{2,0},{4,2},{6,4},{1,7},{3,1},{5,3},{7,5},{8,14},{10,8},{12,... | collective-permute-start | bytes 983048 | tf_op jit(solution)/shard_map/ppermute | solution.py:42
  248.6 9.9 %collective-permute-start.15 = (bf16[640,128]{1,0:T(8,128)(2,1)S(1)}, bf16[640,128]{1,0:T(8,128)(2,1)S(1)}, u32[]{:S(2)}, u32[]{:S(2)}) collective-permute-start(bf16[640,128]{1,0:T(8,128)(2,1)S(1)} %slice_bitcast_fusion.4), channel_id=1, source_target_pairs={{0,2},{2,4},{4,6},{6,0},{1,3},{3,5},{5,7},{7,1},{8,10},{10,12},{12... | collective-permute-start | bytes 491528 | tf_op jit(solution)/shard_map/ppermute | solution.py:42
  251.2 7.7 %collective-permute-start.16 = (bf16[640,128]{1,0:T(8,128)(2,1)S(1)}, bf16[640,128]{1,0:T(8,128)(2,1)S(1)}, u32[]{:S(2)}, u32[]{:S(2)}) collective-permute-start(bf16[640,128]{1,0:T(8,128)(2,1)S(1)} %slice_bitcast_fusion.3), channel_id=1, source_target_pairs={{0,6},{2,0},{4,2},{6,4},{1,7},{3,1},{5,3},{7,5},{8,14},{10,8},{12,... | collective-permute-start | bytes 491528 | tf_op jit(solution)/shard_map/ppermute | solution.py:42
  261.1 40.2 %all-to-all-start.3 = ((bf16[64,80,128]{2,1,0:T(8,128)(2,1)}), bf16[64,80,128]{2,1,0:T(8,128)(2,1)S(1)}, u32[]{:S(2)}, u32[]{:S(2)}) async-start(bf16[64,80,128]{2,1,0:T(8,128)(2,1)} %bitcast.35), calls=%async_computation.3 | async-start | bytes 2621440 | tf_op jit(solution)/shard_map/all_to_all | solution.py:327
  267.5 34.4 %copy-start.11 = (bf16[640,128]{1,0:T(8,128)(2,1)S(1)}, bf16[640,128]{1,0:T(8,128)(2,1)}, u32[]{:S(2)}) copy-start(bf16[640,128]{1,0:T(8,128)(2,1)} %get-tuple-element.43) | copy-start | bytes 491524
  302.6 6.0 %collective-permute-start.17 = (f32[128,512]{1,0:T(8,128)S(1)}, f32[128,512]{1,0:T(8,128)S(1)}, u32[]{:S(2)}, u32[]{:S(2)}) collective-permute-start(f32[128,512]{1,0:T(8,128)S(1)} %slice_select_fusion), channel_id=1, source_target_pairs={{0,1},{1,0},{2,3},{3,2},{4,5},{5,4},{6,7},{7,6},{8,9},{9,8},{10,11... | collective-permute-start | bytes 786440 | tf_op jit(solution)/shard_map/ppermute | solution.py:38
  (8 other events, 24.6 us)
Sparse Core Ops, SparseCore 0:
  53.8 40.6 all-gather.4

commit v3 on v2

--- a/solution.py
+++ b/solution.py
@@ -67,6 +67,7 @@
     near = [shift(near[0], 1), shift(near[1], -1)]
     all_queries = gathered[:, :tokens]
     columns = place_out_weight(gathered[:, tokens:])
+    projection = lax.all_gather(columns, "z", axis=1, tiled=False)
     own = lax.dynamic_slice_in_dim(keys_values, part * rows, rows, axis=0)
     spread = jnp.broadcast_to(own[None], (64, rows, own.shape[1]))
     held = lax.all_to_all(spread, CTX, split_axis=0, concat_axis=0, tiled=True)
@@ -89,8 +90,6 @@
     hi, mid, low = split3(level)
     extra = jnp.stack([hi, mid, low] + [jnp.zeros_like(hi)] * 13, axis=1)
     sent = jnp.concatenate([mean, extra], axis=1)
-    columns, _ = lax.optimization_barrier((columns, sent))
-    projection = lax.all_gather(columns, "z", axis=1, tiled=False)
     came = lax.all_to_all(sent, EXP, split_axis=0, concat_axis=0, tiled=True)
     came_mean = came[:, :tokens].astype(F32)
     came_level = came[:, tokens : tokens + 3].astype(F32)
@@ -271,22 +270,13 @@
     right = shift(hidden, -1)
     far_low = shift(left[0], 1)
     far_high = shift(right[1], -1)
-    block, weight = full(2, 640, 128), full(256, 1024)
-    total = kernel_call(
-        near_output_kernel,
-        [((640, 1024), F32)],
-        1_000_000_000,
-        5_000_000,
-        [block, block, block, weight, weight, weight],
-    )(hidden, left, right, part(0), part(3), part(1))[0]
-    out = kernel_call(
-        final_kernel,
-        [((5120, 128), BF16)],
-        340_000_000,
-        5_000_000,
-        [full(640, 1024), full(640, 128), full(640, 128), weight],
-    )(total, far_low, far_high, part(2))[0]
-    return out.reshape(64, 80, 128)
+    def product(block, k):
+        rows = part(k)
+        return dot(block[0], rows[:128]) + dot(block[1], rows[128:])
+
+    total = product(hidden, 0) + product(left, 3) + product(right, 1)
+    total = total + product((far_low, far_high), 2)
+    return total.astype(BF16).reshape(64, 80, 128)
 
 
 def per_device(

time: 318 us -> 313 us (0.984)
  blocking collectives: 44.4 us -> 34.2 us
  starting transfers between devices: 109 us -> 119 us
  matrix products: 5.07 us -> 9.52 us
  Pallas kernels: 12.7 us -> 8.28 us
    all_to_all x1, starting transfers between devices: 6.38 us -> 22.1 us  [per_device(): lax.all_to_all(expert_out, CTX, split_axis=0, concat_axis=0, tiled=True)]
    all_gather x1, blocking collectives: 27.5 us -> 17.3 us  [attention_rows(): attention = lax.all_gather(mine, EXP, axis=0, tiled=False)]
    all_to_all x1, waiting for transfers between devices: 24.2 us -> 16.7 us  [per_device(): lax.all_to_all(outgoing, CTX, split_axis=0, concat_axis=0, tiled=True)]
    all_to_all x1, starting transfers between devices: 17 us -> 10.5 us  [per_device(): lax.all_to_all(outgoing, CTX, split_axis=0, concat_axis=0, tiled=True)]
    all_to_all x1, waiting for transfers between devices: 10.3 us -> 14.7 us  [attention_rows(): came = lax.all_to_all(sent, EXP, split_axis=0, concat_axis=0, tiled=True)]
    dot_general x0 -> x8, matrix products: none -> 4.45 us  [dot(): return jnp.dot(left, right, preferred_element_type=F32)]
    pallas_call x2 -> x0, Pallas kernels: 4.32 us -> none  [the longest x1 2.18 us: expert_outputs(): kernel_call(near_output_kernel, [((640, 1024), F32)], 1000000000, 5000000...]
  transfers between devices with their start and end apart: 23 -> 23, of which waited for: 11 -> 12; matrix products, arithmetic and copies ran while one was open for 7% -> 8% of each run, Pallas kernels for 2% -> 2%
where the time goes in v3:
time: 313 us; the launch traced here: 312 us
  starting transfers between devices  119 us (38%)
  waiting for transfers between devices  102 us (33%)
  blocking collectives  34.2 us (11%)
  other arithmetic  14.7 us (5%)
  between operations  14.2 us (5%)
  local copies, waits for them, and re-layouts  10.4 us (3%)
  matrix products  9.52 us (3%)
  Pallas kernels  8.28 us (3%)
    ppermute x13, starting transfers between devices, shift(): return lax.ppermute(block, 'y_hi', [(i, (i + step) % 4) for i in range(4)])  49.7 us
    ppermute x13, waiting for transfers between devices, shift(): return lax.ppermute(block, 'y_hi', [(i, (i + step) % 4) for i in range(4)])  34.8 us
    all_to_all x1, waiting for transfers between devices, per_device(): lax.all_to_all(expert_out, CTX, split_axis=0, concat_axis=0, tiled=True)  34 us
    all_to_all x1, starting transfers between devices, per_device(): lax.all_to_all(expert_out, CTX, split_axis=0, concat_axis=0, tiled=True)  22.1 us
    all_gather x1, blocking collectives, attention_rows(): attention = lax.all_gather(mine, EXP, axis=0, tiled=False)  17.3 us
    all_gather x1, blocking collectives, attention_rows(): lax.all_gather(jnp.concatenate([queries, out_weight.T], axis=0), EXP, axi...  16.9 us
    all_to_all x1, waiting for transfers between devices, per_device(): lax.all_to_all(outgoing, CTX, split_axis=0, concat_axis=0, tiled=True)  16.7 us
    all_to_all x1, starting transfers between devices, attention_rows(): held = lax.all_to_all(spread, CTX, split_axis=0, concat_axis=0, tiled=True)  15.3 us
  transfers between devices with their start and end apart: 23, of which 12 were waited for; matrix products, arithmetic and copies ran while one was open for 8% of the time, Pallas kernels for 2%

profile of v3, /device:TPU:1, one launch (start us, length us, event | category | flops | bytes accessed | tf_op | source)
XLA Modules:
  0.0 311.9 jit_solution(5737963875784583777)
XLA Ops:
  8.2 15.3 %all-to-all-start = ((bf16[64,16,256]{2,1,0:T(8,128)(2,1)}), bf16[64,16,256]{2,1,0:T(8,128)(2,1)S(1)}, u32[]{:S(2)}, u32[]{:S(2)}) async-start(bf16[64,16,256]{2,1,0:T(8,128)(2,1)} %broadcast_in_dim.83), calls=%async_computation | async-start | bytes 1048576 | tf_op jit(solution)/shard_map/all_to_all | solution.py:73
  24.5 2.7 fusion.17
  27.2 16.9 %all-gather = bf16[1536,128]{1,0:T(8,128)(2,1)S(1)} all-gather(bf16[192,128]{1,0:T(8,128)(2,1)S(1)} %pad_maximum_fusion.1), channel_id=2, replica_groups=mesh['y_lo'=2,'x'=4,'z'=8,'y_hi'=4,'core'=2] {'y_hi','core'}, dimensions={0}, use_global_device_ids=true | all-gather | bytes 442368 | tf_op jit(solution)/shard_map/all_gather | solution.py:63
  44.1 3.3 %collective-permute-start.2 = (bf16[8,64,128]{2,1,0:T(8,128)(2,1)S(1)}, bf16[8,64,128]{2,1,0:T(8,128)(2,1)S(1)}, u32[]{:S(2)}, u32[]{:S(2)}) collective-permute-start(bf16[8,64,128]{2,1,0:T(8,128)(2,1)S(1)} %slice.109), channel_id=1, source_target_pairs={{0,0},{1,64},{2,128},{3,192},{4,256},{5,320},{6,384},{7,448},{64,1... | collective-permute-start | bytes 393224 | tf_op jit(solution)/shard_map/ppermute | solution.py:34
  47.4 5.2 %collective-permute-start = (bf16[1024,256]{1,0:T(8,128)(2,1)}, bf16[1024,256]{1,0:T(8,128)(2,1)S(1)}, u32[]{:S(2)}, u32[]{:S(2)}) collective-permute-start(bf16[1024,256]{1,0:T(8,128)(2,1)} %get-tuple-element.24), channel_id=1, source_target_pairs={{0,2},{2,4},{4,6},{6,0},{1,3},{3,5},{5,7},{7,1},{8,10},{10,12},{12... | collective-permute-start | bytes 1572872 | tf_op jit(solution)/shard_map/ppermute | solution.py:42
  52.6 4.5 %collective-permute-start.1 = (bf16[1024,256]{1,0:T(8,128)(2,1)}, bf16[1024,256]{1,0:T(8,128)(2,1)S(1)}, u32[]{:S(2)}, u32[]{:S(2)}) collective-permute-start(bf16[1024,256]{1,0:T(8,128)(2,1)} %get-tuple-element.25), channel_id=1, source_target_pairs={{0,6},{2,0},{4,2},{6,4},{1,7},{3,1},{5,3},{7,5},{8,14},{10,8},{12,... | collective-permute-start | bytes 1572872 | tf_op jit(solution)/shard_map/ppermute | solution.py:42
  63.8 5.1 %all-to-all-start.1 = ((bf16[8,144,128]{2,1,0:T(8,128)(2,1)}), bf16[8,144,128]{2,1,0:T(8,128)(2,1)S(1)}, u32[]{:S(2)}, u32[]{:S(2)}) async-start(bf16[8,144,128]{2,1,0:T(8,128)(2,1)} %concatenate.36), calls=%async_computation.1 | async-start | bytes 589824 | tf_op jit(solution)/shard_map/all_to_all | solution.py:93
  69.5 14.7 %all-to-all-done.1 = bf16[8,144,128]{2,1,0:T(8,128)(2,1)S(1)} async-done(((bf16[8,144,128]{2,1,0:T(8,128)(2,1)}), bf16[8,144,128]{2,1,0:T(8,128)(2,1)S(1)}, u32[]{:S(2)}, u32[]{:S(2)}) %all-to-all-start.1) | async-done | bytes 294944 | tf_op jit(solution)/shard_map/all_to_all | solution.py:93
  84.6 17.3 %all-gather.1 = bf16[1024,128]{1,0:T(8,128)(2,1)S(1)} all-gather(bf16[128,128]{1,0:T(8,128)(2,1)S(1)} %multiply_reduce_fusion), channel_id=3, replica_groups=mesh['y_lo'=2,'x'=4,'z'=8,'y_hi'=4,'core'=2] {'y_hi','core'}, dimensions={0}, use_global_device_ids=true | all-gather | bytes 294912 | tf_op jit(solution)/shard_map/all_gather | solution.py:101
  105.8 6.9 %collective-permute-start.4 = (bf16[1024,256]{1,0:T(8,128)(2,1)}, bf16[1024,256]{1,0:T(8,128)(2,1)}, u32[]{:S(2)}, u32[]{:S(2)}) collective-permute-start(bf16[1024,256]{1,0:T(8,128)(2,1)} %get-tuple-element.30), channel_id=1, source_target_pairs={{0,4},{2,6},{4,0},{6,2},{1,5},{3,7},{5,1},{7,3},{8,12},{10,14},{12... | collective-permute-start | bytes 1572872 | tf_op jit(solution)/shard_map/ppermute | solution.py:42
  115.5 10.5 %all-to-all-start.2 = ((bf16[64,80,128]{2,1,0:T(8,128)(2,1)}), bf16[64,80,128]{2,1,0:T(8,128)(2,1)}, u32[]{:S(2)}, u32[]{:S(2)}) async-start(bf16[64,80,128]{2,1,0:T(8,128)(2,1)} %reshape.209), calls=%async_computation.2 | async-start | bytes 2621440 | tf_op jit(solution)/shard_map/all_to_all | solution.py:313
  126.0 5.0 %collective-permute-done.4 = bf16[1024,256]{1,0:T(8,128)(2,1)} collective-permute-done((bf16[1024,256]{1,0:T(8,128)(2,1)}, bf16[1024,256]{1,0:T(8,128)(2,1)}, u32[]{:S(2)}, u32[]{:S(2)}) %collective-permute-start.4) | collective-permute-done | bytes 524320 | tf_op jit(solution)/shard_map/ppermute | solution.py:42
  132.5 3.9 %collective-permute-start.5 = (bf16[4,1024,256]{2,1,0:T(8,128)(2,1)S(1)}, bf16[4,1024,256]{2,1,0:T(8,128)(2,1)}, u32[]{:S(2)}, u32[]{:S(2)}) collective-permute-start(bf16[4,1024,256]{2,1,0:T(8,128)(2,1)S(1)} %pad_maximum_fusion), channel_id=1, source_target_pairs={{0,1},{1,0},{2,3},{3,2},{4,5},{5,4},{6,7},{7,6},{8,9},{9,8},{10,11... | collective-permute-start | bytes 6291464 | tf_op jit(solution)/shard_map/ppermute | solution.py:38
  140.2 2.9 broadcast_select_fusion.2
  143.1 16.7 %all-to-all-done.2 = bf16[64,80,128]{2,1,0:T(8,128)(2,1)} async-done(((bf16[64,80,128]{2,1,0:T(8,128)(2,1)}), bf16[64,80,128]{2,1,0:T(8,128)(2,1)}, u32[]{:S(2)}, u32[]{:S(2)}) %all-to-all-start.2) | async-done | bytes 1310752 | tf_op jit(solution)/shard_map/all_to_all | solution.py:313
  159.9 5.3 %shard_map.100 = (bf16[640,1024]{1,0:T(8,128)(2,1)}, bf16[16,256]{1,0:T(8,128)(2,1)}, bf16[656,256]{1,0:T(8,128)(2,1)}, bf16[640,256]{1,0:T(8,128)(2,1)}) custom-call(bf16[5120,128]{1,0:T(8,128)(2,1)} %bitcast.22.arrived, f32[1,1024]{1,0:T(1,128)} %bitcast.120, bf16[1024,256]{1,0:T(8,128)(2,1)} %get-tuple-element.59.low_weight, ...), custom_call_target="tpu_custom_call" | custom-call | flops 680000000 | bytes 4500000 | tf_op jit(solution)/shard_map/pallas_call | solution.py:208
  165.1 3.0 collective-permute-start.10
  170.8 3.2 %collective-permute-start.6 = (bf16[656,256]{1,0:T(8,128)(2,1)S(1)}, bf16[656,256]{1,0:T(8,128)(2,1)S(1)}, u32[]{:S(2)}, u32[]{:S(2)}) collective-permute-start(bf16[656,256]{1,0:T(8,128)(2,1)S(1)} %copy-done.12), channel_id=1, source_target_pairs={{0,2},{2,4},{4,6},{6,0},{1,3},{3,5},{5,7},{7,1},{8,10},{10,12},{12... | collective-permute-start | bytes 1007624 | tf_op jit(solution)/shard_map/ppermute | solution.py:42
  175.6 3.3 %collective-permute-start.8 = (bf16[656,256]{1,0:T(8,128)(2,1)S(1)}, bf16[656,256]{1,0:T(8,128)(2,1)S(1)}, u32[]{:S(2)}, u32[]{:S(2)}) collective-permute-start(bf16[656,256]{1,0:T(8,128)(2,1)S(1)} %get-tuple-element.37), channel_id=1, source_target_pairs={{0,2},{2,4},{4,6},{6,0},{1,3},{3,5},{5,7},{7,1},{8,10},{10,12},{12... | collective-permute-start | bytes 1007624 | tf_op jit(solution)/shard_map/ppermute | solution.py:42
  178.9 4.1 %collective-permute-start.9 = (bf16[656,256]{1,0:T(8,128)(2,1)S(1)}, bf16[656,256]{1,0:T(8,128)(2,1)S(1)}, u32[]{:S(2)}, u32[]{:S(2)}) collective-permute-start(bf16[656,256]{1,0:T(8,128)(2,1)S(1)} %get-tuple-element.38), channel_id=1, source_target_pairs={{0,6},{2,0},{4,2},{6,4},{1,7},{3,1},{5,3},{7,5},{8,14},{10,8},{12,... | collective-permute-start | bytes 1007624 | tf_op jit(solution)/shard_map/ppermute | solution.py:42
  183.1 3.0 collective-permute-start.11
  186.2 3.2 %collective-permute-start.7 = (bf16[656,256]{1,0:T(8,128)(2,1)S(1)}, bf16[656,256]{1,0:T(8,128)(2,1)S(1)}, u32[]{:S(2)}, u32[]{:S(2)}) collective-permute-start(bf16[656,256]{1,0:T(8,128)(2,1)S(1)} %add_convert_fusion.1), channel_id=1, source_target_pairs={{0,2},{2,4},{4,6},{6,0},{1,3},{3,5},{5,7},{7,1},{8,10},{10,12},{12... | collective-permute-start | bytes 1007624 | tf_op jit(solution)/shard_map/ppermute | solution.py:42
  192.1 3.8 %collective-permute-done.9.right_low = bf16[656,256]{1,0:T(8,128)(2,1)S(1)} collective-permute-done((bf16[656,256]{1,0:T(8,128)(2,1)S(1)}, bf16[656,256]{1,0:T(8,128)(2,1)S(1)}, u32[]{:S(2)}, u32[]{:S(2)}) %collective-permute-start.9) | collective-permute-done | bytes 335904 | tf_op jit(solution)/shard_map/ppermute | solution.py:42
  195.9 15.3 %collective-permute-done.11.right_high = bf16[640,256]{1,0:T(8,128)(2,1)S(1)} collective-permute-done((bf16[640,256]{1,0:T(8,128)(2,1)S(1)}, bf16[640,256]{1,0:T(8,128)(2,1)S(1)}, u32[]{:S(2)}, u32[]{:S(2)}) %collective-permute-start.11) | collective-permute-done | bytes 327712 | tf_op jit(solution)/shard_map/ppermute | solution.py:42
  211.8 3.5 %collective-permute-start.14 = (bf16[2,640,128]{2,1,0:T(8,128)(2,1)S(1)}, bf16[2,640,128]{2,1,0:T(8,128)(2,1)S(1)}, u32[]{:S(2)}, u32[]{:S(2)}) collective-permute-start(bf16[2,640,128]{2,1,0:T(8,128)(2,1)S(1)} %shard_map.103), channel_id=1, source_target_pairs={{0,6},{2,0},{4,2},{6,4},{1,7},{3,1},{5,3},{7,5},{8,14},{10,8},{12,... | collective-permute-start | bytes 983048 | tf_op jit(solution)/shard_map/ppermute | solution.py:42
  215.3 2.6 collective-permute-start.13
  221.5 3.8 %collective-permute-start.16 = (bf16[640,128]{1,0:T(8,128)(2,1)S(1)}, bf16[640,128]{1,0:T(8,128)(2,1)S(1)}, u32[]{:S(2)}, u32[]{:S(2)}) collective-permute-start(bf16[640,128]{1,0:T(8,128)(2,1)S(1)} %slice_bitcast_fusion.3), channel_id=1, source_target_pairs={{0,6},{2,0},{4,2},{6,4},{1,7},{3,1},{5,3},{7,5},{8,14},{10,8},{12,... | collective-permute-start | bytes 491528 | tf_op jit(solution)/shard_map/ppermute | solution.py:42
  225.3 3.4 %collective-permute-start.15 = (bf16[640,128]{1,0:T(8,128)(2,1)S(1)}, bf16[640,128]{1,0:T(8,128)(2,1)S(1)}, u32[]{:S(2)}, u32[]{:S(2)}) collective-permute-start(bf16[640,128]{1,0:T(8,128)(2,1)S(1)} %slice_bitcast_fusion.8), channel_id=1, source_target_pairs={{0,2},{2,4},{4,6},{6,0},{1,3},{3,5},{5,7},{7,1},{8,10},{10,12},{12... | collective-permute-start | bytes 491528 | tf_op jit(solution)/shard_map/ppermute | solution.py:42
  230.7 5.8 %collective-permute-done.16 = bf16[640,128]{1,0:T(8,128)(2,1)S(1)} collective-permute-done((bf16[640,128]{1,0:T(8,128)(2,1)S(1)}, bf16[640,128]{1,0:T(8,128)(2,1)S(1)}, u32[]{:S(2)}, u32[]{:S(2)}) %collective-permute-start.16) | collective-permute-done | bytes 163872 | tf_op jit(solution)/shard_map/ppermute | solution.py:42
  241.1 22.1 %all-to-all-start.3 = ((bf16[64,80,128]{2,1,0:T(8,128)(2,1)}), bf16[64,80,128]{2,1,0:T(8,128)(2,1)S(1)}, u32[]{:S(2)}, u32[]{:S(2)}) async-start(bf16[64,80,128]{2,1,0:T(8,128)(2,1)} %reshape.211), calls=%async_computation.3 | async-start | bytes 2621440 | tf_op jit(solution)/shard_map/all_to_all | solution.py:317
  263.3 34.0 %all-to-all-done.3 = bf16[64,80,128]{2,1,0:T(8,128)(2,1)S(1)} async-done(((bf16[64,80,128]{2,1,0:T(8,128)(2,1)}), bf16[64,80,128]{2,1,0:T(8,128)(2,1)S(1)}, u32[]{:S(2)}, u32[]{:S(2)}) %all-to-all-start.3) | async-done | bytes 1310752 | tf_op jit(solution)/shard_map/all_to_all | solution.py:317
  298.6 4.5 %collective-permute-start.17 = (f32[128,512]{1,0:T(8,128)S(1)}, f32[128,512]{1,0:T(8,128)S(1)}, u32[]{:S(2)}, u32[]{:S(2)}) collective-permute-start(f32[128,512]{1,0:T(8,128)S(1)} %slice_select_fusion), channel_id=1, source_target_pairs={{0,1},{1,0},{2,3},{3,2},{4,5},{5,4},{6,7},{7,6},{8,9},{9,8},{10,11... | collective-permute-start | bytes 786440 | tf_op jit(solution)/shard_map/ppermute | solution.py:38
  (115 shorter events, 42.7 us)
Async XLA Ops:
  8.2 49.8 %all-to-all-start = ((bf16[64,16,256]{2,1,0:T(8,128)(2,1)}), bf16[64,16,256]{2,1,0:T(8,128)(2,1)S(1)}, u32[]{:S(2)}, u32[]{:S(2)}) async-start(bf16[64,16,256]{2,1,0:T(8,128)(2,1)} %broadcast_in_dim.83), calls=%async_computation | async-start | bytes 1048576 | tf_op jit(solution)/shard_map/all_to_all | solution.py:73
  23.6 78.3 %all-gather.5.cloned.1.call-start = ((), (), s32[]{:S(2)}) async-start(), calls=%async_computation.4 | async-start | bytes 1179648 | tf_op jit(solution)/shard_map/all_gather | solution.py:70
  44.1 13.2 %collective-permute-start.2 = (bf16[8,64,128]{2,1,0:T(8,128)(2,1)S(1)}, bf16[8,64,128]{2,1,0:T(8,128)(2,1)S(1)}, u32[]{:S(2)}, u32[]{:S(2)}) collective-permute-start(bf16[8,64,128]{2,1,0:T(8,128)(2,1)S(1)} %slice.109), channel_id=1, source_target_pairs={{0,0},{1,64},{2,128},{3,192},{4,256},{5,320},{6,384},{7,448},{64,1... | collective-permute-start | bytes 393224 | tf_op jit(solution)/shard_map/ppermute | solution.py:34
  47.4 37.2 %collective-permute-start = (bf16[1024,256]{1,0:T(8,128)(2,1)}, bf16[1024,256]{1,0:T(8,128)(2,1)S(1)}, u32[]{:S(2)}, u32[]{:S(2)}) collective-permute-start(bf16[1024,256]{1,0:T(8,128)(2,1)} %get-tuple-element.24), channel_id=1, source_target_pairs={{0,2},{2,4},{4,6},{6,0},{1,3},{3,5},{5,7},{7,1},{8,10},{10,12},{12... | collective-permute-start | bytes 1572872 | tf_op jit(solution)/shard_map/ppermute | solution.py:42
  52.6 31.9 %collective-permute-start.1 = (bf16[1024,256]{1,0:T(8,128)(2,1)}, bf16[1024,256]{1,0:T(8,128)(2,1)S(1)}, u32[]{:S(2)}, u32[]{:S(2)}) collective-permute-start(bf16[1024,256]{1,0:T(8,128)(2,1)} %get-tuple-element.25), channel_id=1, source_target_pairs={{0,6},{2,0},{4,2},{6,4},{1,7},{3,1},{5,3},{7,5},{8,14},{10,8},{12,... | collective-permute-start | bytes 1572872 | tf_op jit(solution)/shard_map/ppermute | solution.py:42
  60.4 8.7 %copy-start.10 = (s32[128,8]{0,1:T(8,128)S(1)}, s32[128,8]{0,1:T(8,128)}, u32[]{:S(2)}) copy-start(s32[128,8]{0,1:T(8,128)} %param.15) | copy-start | bytes 12292
  60.4 8.7 %copy-start.11 = (f32[128,8]{0,1:T(8,128)S(1)}, f32[128,8]{0,1:T(8,128)}, u32[]{:S(2)}) copy-start(f32[128,8]{0,1:T(8,128)} %param.16) | copy-start | bytes 12292
  63.8 20.5 %all-to-all-start.1 = ((bf16[8,144,128]{2,1,0:T(8,128)(2,1)}), bf16[8,144,128]{2,1,0:T(8,128)(2,1)S(1)}, u32[]{:S(2)}, u32[]{:S(2)}) async-start(bf16[8,144,128]{2,1,0:T(8,128)(2,1)} %concatenate.36), calls=%async_computation.1 | async-start | bytes 589824 | tf_op jit(solution)/shard_map/all_to_all | solution.py:93
  69.2 34.5 %copy-start.9 = (bf16[128,512]{1,0:T(8,128)(2,1)S(1)}, bf16[128,512]{1,0:T(8,128)(2,1)}, u32[]{:S(2)}) copy-start(bf16[128,512]{1,0:T(8,128)(2,1)} %param.10) | copy-start | bytes 393220
  84.5 29.5 %copy-start.4 = (bf16[1024,256]{1,0:T(8,128)(2,1)}, bf16[1024,256]{1,0:T(8,128)(2,1)S(1)}, u32[]{:S(2)}) copy-start(bf16[1024,256]{1,0:T(8,128)(2,1)S(1)} %collective-permute-done.1) | copy-start | bytes 1572868
  103.7 9.8 %copy-start.5 = (bf16[128,512]{1,0:T(8,128)(2,1)}, bf16[128,512]{1,0:T(8,128)(2,1)S(1)}, u32[]{:S(2)}) copy-start(bf16[128,512]{1,0:T(8,128)(2,1)S(1)} %add_convert_fusion.4) | copy-start | bytes 393220
  103.7 9.8 %collective-permute-start.3 = (bf16[128,512]{1,0:T(8,128)(2,1)S(1)}, bf16[128,512]{1,0:T(8,128)(2,1)S(1)}, u32[]{:S(2)}, u32[]{:S(2)}) collective-permute-start(bf16[128,512]{1,0:T(8,128)(2,1)S(1)} %add_convert_fusion.4), channel_id=1, source_target_pairs={{0,1},{1,0},{2,3},{3,2},{4,5},{5,4},{6,7},{7,6},{8,9},{9,8},{10,11... | collective-permute-start | bytes 393224 | tf_op jit(solution)/shard_map/ppermute | solution.py:38
  105.8 25.2 %collective-permute-start.4 = (bf16[1024,256]{1,0:T(8,128)(2,1)}, bf16[1024,256]{1,0:T(8,128)(2,1)}, u32[]{:S(2)}, u32[]{:S(2)}) collective-permute-start(bf16[1024,256]{1,0:T(8,128)(2,1)} %get-tuple-element.30), channel_id=1, source_target_pairs={{0,4},{2,6},{4,0},{6,2},{1,5},{3,7},{5,1},{7,3},{8,12},{10,14},{12... | collective-permute-start | bytes 1572872 | tf_op jit(solution)/shard_map/ppermute | solution.py:42
  115.5 44.4 %all-to-all-start.2 = ((bf16[64,80,128]{2,1,0:T(8,128)(2,1)}), bf16[64,80,128]{2,1,0:T(8,128)(2,1)}, u32[]{:S(2)}, u32[]{:S(2)}) async-start(bf16[64,80,128]{2,1,0:T(8,128)(2,1)} %reshape.209), calls=%async_computation.2 | async-start | bytes 2621440 | tf_op jit(solution)/shard_map/all_to_all | solution.py:313
  132.5 7.8 %collective-permute-start.5 = (bf16[4,1024,256]{2,1,0:T(8,128)(2,1)S(1)}, bf16[4,1024,256]{2,1,0:T(8,128)(2,1)}, u32[]{:S(2)}, u32[]{:S(2)}) collective-permute-start(bf16[4,1024,256]{2,1,0:T(8,128)(2,1)S(1)} %pad_maximum_fusion), channel_id=1, source_target_pairs={{0,1},{1,0},{2,3},{3,2},{4,5},{5,4},{6,7},{7,6},{8,9},{9,8},{10,11... | collective-permute-start | bytes 6291464 | tf_op jit(solution)/shard_map/ppermute | solution.py:38
  136.3 31.8 %collective-permute-start.12 = (bf16[1024,512]{1,0:T(8,128)(2,1)}, bf16[1024,512]{1,0:T(8,128)(2,1)}, u32[]{:S(2)}, u32[]{:S(2)}) collective-permute-start(bf16[1024,512]{1,0:T(8,128)(2,1)} %bitcast.33), channel_id=1, source_target_pairs={{0,1},{1,0},{2,3},{3,2},{4,5},{5,4},{6,7},{7,6},{8,9},{9,8},{10,11... | collective-permute-start | bytes 3145736 | tf_op jit(solution)/shard_map/ppermute | solution.py:38
  165.1 17.9 %collective-permute-start.10 = (bf16[640,256]{1,0:T(8,128)(2,1)}, bf16[640,256]{1,0:T(8,128)(2,1)S(1)}, u32[]{:S(2)}, u32[]{:S(2)}) collective-permute-start(bf16[640,256]{1,0:T(8,128)(2,1)} %get-tuple-element.40), channel_id=1, source_target_pairs={{0,6},{2,0},{4,2},{6,4},{1,7},{3,1},{5,3},{7,5},{8,14},{10,8},{12,... | collective-permute-start | bytes 983048 | tf_op jit(solution)/shard_map/ppermute | solution.py:42
  169.8 4.2 %copy-start.2 = (bf16[640,1024]{1,0:T(8,128)(2,1)S(1)}, bf16[640,1024]{1,0:T(8,128)(2,1)}, u32[]{:S(2)}) copy-start(bf16[640,1024]{1,0:T(8,128)(2,1)} %get-tuple-element.33.scaled) | copy-start | bytes 3932164
  170.8 15.3 %collective-permute-start.6 = (bf16[656,256]{1,0:T(8,128)(2,1)S(1)}, bf16[656,256]{1,0:T(8,128)(2,1)S(1)}, u32[]{:S(2)}, u32[]{:S(2)}) collective-permute-start(bf16[656,256]{1,0:T(8,128)(2,1)S(1)} %copy-done.12), channel_id=1, source_target_pairs={{0,2},{2,4},{4,6},{6,0},{1,3},{3,5},{5,7},{7,1},{8,10},{10,12},{12... | collective-permute-start | bytes 1007624 | tf_op jit(solution)/shard_map/ppermute | solution.py:42
  175.6 16.5 %collective-permute-start.8 = (bf16[656,256]{1,0:T(8,128)(2,1)S(1)}, bf16[656,256]{1,0:T(8,128)(2,1)S(1)}, u32[]{:S(2)}, u32[]{:S(2)}) collective-permute-start(bf16[656,256]{1,0:T(8,128)(2,1)S(1)} %get-tuple-element.37), channel_id=1, source_target_pairs={{0,2},{2,4},{4,6},{6,0},{1,3},{3,5},{5,7},{7,1},{8,10},{10,12},{12... | collective-permute-start | bytes 1007624 | tf_op jit(solution)/shard_map/ppermute | solution.py:42
  178.9 17.0 %collective-permute-start.9 = (bf16[656,256]{1,0:T(8,128)(2,1)S(1)}, bf16[656,256]{1,0:T(8,128)(2,1)S(1)}, u32[]{:S(2)}, u32[]{:S(2)}) collective-permute-start(bf16[656,256]{1,0:T(8,128)(2,1)S(1)} %get-tuple-element.38), channel_id=1, source_target_pairs={{0,6},{2,0},{4,2},{6,4},{1,7},{3,1},{5,3},{7,5},{8,14},{10,8},{12,... | collective-permute-start | bytes 1007624 | tf_op jit(solution)/shard_map/ppermute | solution.py:42
  183.1 28.1 %collective-permute-start.11 = (bf16[640,256]{1,0:T(8,128)(2,1)S(1)}, bf16[640,256]{1,0:T(8,128)(2,1)S(1)}, u32[]{:S(2)}, u32[]{:S(2)}) collective-permute-start(bf16[640,256]{1,0:T(8,128)(2,1)S(1)} %add_convert_fusion.2), channel_id=1, source_target_pairs={{0,6},{2,0},{4,2},{6,4},{1,7},{3,1},{5,3},{7,5},{8,14},{10,8},{12,... | collective-permute-start | bytes 983048 | tf_op jit(solution)/shard_map/ppermute | solution.py:42
  186.2 25.0 %collective-permute-start.7 = (bf16[656,256]{1,0:T(8,128)(2,1)S(1)}, bf16[656,256]{1,0:T(8,128)(2,1)S(1)}, u32[]{:S(2)}, u32[]{:S(2)}) collective-permute-start(bf16[656,256]{1,0:T(8,128)(2,1)S(1)} %add_convert_fusion.1), channel_id=1, source_target_pairs={{0,2},{2,4},{4,6},{6,0},{1,3},{3,5},{5,7},{7,1},{8,10},{10,12},{12... | collective-permute-start | bytes 1007624 | tf_op jit(solution)/shard_map/ppermute | solution.py:42
  211.8 9.6 %collective-permute-start.14 = (bf16[2,640,128]{2,1,0:T(8,128)(2,1)S(1)}, bf16[2,640,128]{2,1,0:T(8,128)(2,1)S(1)}, u32[]{:S(2)}, u32[]{:S(2)}) collective-permute-start(bf16[2,640,128]{2,1,0:T(8,128)(2,1)S(1)} %shard_map.103), channel_id=1, source_target_pairs={{0,6},{2,0},{4,2},{6,4},{1,7},{3,1},{5,3},{7,5},{8,14},{10,8},{12,... | collective-permute-start | bytes 983048 | tf_op jit(solution)/shard_map/ppermute | solution.py:42
  215.3 9.9 %collective-permute-start.13 = (bf16[2,640,128]{2,1,0:T(8,128)(2,1)S(1)}, bf16[2,640,128]{2,1,0:T(8,128)(2,1)S(1)}, u32[]{:S(2)}, u32[]{:S(2)}) collective-permute-start(bf16[2,640,128]{2,1,0:T(8,128)(2,1)S(1)} %shard_map.103), channel_id=1, source_target_pairs={{0,2},{2,4},{4,6},{6,0},{1,3},{3,5},{5,7},{7,1},{8,10},{10,12},{12... | collective-permute-start | bytes 983048 | tf_op jit(solution)/shard_map/ppermute | solution.py:42
  221.5 15.0 %collective-permute-start.16 = (bf16[640,128]{1,0:T(8,128)(2,1)S(1)}, bf16[640,128]{1,0:T(8,128)(2,1)S(1)}, u32[]{:S(2)}, u32[]{:S(2)}) collective-permute-start(bf16[640,128]{1,0:T(8,128)(2,1)S(1)} %slice_bitcast_fusion.3), channel_id=1, source_target_pairs={{0,6},{2,0},{4,2},{6,4},{1,7},{3,1},{5,3},{7,5},{8,14},{10,8},{12,... | collective-permute-start | bytes 491528 | tf_op jit(solution)/shard_map/ppermute | solution.py:42
  225.3 13.3 %collective-permute-start.15 = (bf16[640,128]{1,0:T(8,128)(2,1)S(1)}, bf16[640,128]{1,0:T(8,128)(2,1)S(1)}, u32[]{:S(2)}, u32[]{:S(2)}) collective-permute-start(bf16[640,128]{1,0:T(8,128)(2,1)S(1)} %slice_bitcast_fusion.8), channel_id=1, source_target_pairs={{0,2},{2,4},{4,6},{6,0},{1,3},{3,5},{5,7},{7,1},{8,10},{10,12},{12... | collective-permute-start | bytes 491528 | tf_op jit(solution)/shard_map/ppermute | solution.py:42
  241.1 56.8 %copy-start.7 = (bf16[640,128]{1,0:T(8,128)(2,1)S(1)}, bf16[640,128]{1,0:T(8,128)(2,1)}, u32[]{:S(2)}) copy-start(bf16[640,128]{1,0:T(8,128)(2,1)} %get-tuple-element.41) | copy-start | bytes 491524
  241.1 56.2 %all-to-all-start.3 = ((bf16[64,80,128]{2,1,0:T(8,128)(2,1)}), bf16[64,80,128]{2,1,0:T(8,128)(2,1)S(1)}, u32[]{:S(2)}, u32[]{:S(2)}) async-start(bf16[64,80,128]{2,1,0:T(8,128)(2,1)} %reshape.211), calls=%async_computation.3 | async-start | bytes 2621440 | tf_op jit(solution)/shard_map/all_to_all | solution.py:317
  297.9 6.4 %copy-start.6 = (bf16[128,512]{1,0:T(8,128)(2,1)S(1)}, bf16[128,512]{1,0:T(8,128)(2,1)}, u32[]{:S(2)}) copy-start(bf16[128,512]{1,0:T(8,128)(2,1)} %copy-done.5) | copy-start | bytes 393220
  297.9 7.1 %copy-start.1 = (bf16[128,256]{1,0:T(8,128)(2,1)S(1)}, bf16[128,256]{1,0:T(8,128)(2,1)}, u32[]{:S(2)}) copy-start(bf16[128,256]{1,0:T(8,128)(2,1)} %param.12) | copy-start | bytes 196612
  298.6 5.6 %collective-permute-start.17 = (f32[128,512]{1,0:T(8,128)S(1)}, f32[128,512]{1,0:T(8,128)S(1)}, u32[]{:S(2)}, u32[]{:S(2)}) collective-permute-start(f32[128,512]{1,0:T(8,128)S(1)} %slice_select_fusion), channel_id=1, source_target_pairs={{0,1},{1,0},{2,3},{3,2},{4,5},{5,4},{6,7},{7,6},{8,9},{9,8},{10,11... | collective-permute-start | bytes 786440 | tf_op jit(solution)/shard_map/ppermute | solution.py:38
  (4 other events, 6.7 us)
Sparse Core Ops, SparseCore 0:
  58.1 38.6 all-gather.4

commit v4 on v3

--- a/solution.py
+++ b/solution.py
@@ -145,16 +145,12 @@
     tiles = []
     for i in range(5):
         here = slice(128 * i, 128 * i + 128)
-        rows = arrived[1024 * i : 1024 * i + 1024, :].astype(F32)
-        rows = rows.reshape(128, 8, 128).reshape(128, 1024)
-        block = (rows * gain[...]).astype(BF16)
+        rows = arrived[1024 * i : 1024 * i + 1024, :].astype(F32).reshape(128, 8, 128)
+        total = jnp.sum(rows * rows, axis=1)
+        block = (rows.reshape(128, 1024) * gain[...]).astype(BF16)
         scaled[here, :] = block
         far_low[here, :] = dot(block, low_weight[...]).astype(BF16)
         far_high[here, :] = dot(block, high_weight[...]).astype(BF16)
-        square = rows * rows
-        total = square[:, :128]
-        for j in range(1, 8):
-            total = total + square[:, 128 * j : 128 * j + 128]
         total = jnp.sum(total.T, axis=0, keepdims=True)
         spread = total * 65537.0
         high = spread - (spread - total)
@@ -203,7 +199,7 @@
             hidden[half, here, :] = value.astype(BF16)
 
 
-def expert_hidden(arrived, gain, low, high):
+def expert_hidden(arrived, gain, low, high, down):
     weight = full(1024, 256)
     scaled, squares, far_low, far_high = kernel_call(
         receive_kernel,
@@ -222,6 +218,8 @@
         5_500_000,
         [full(640, 1024), full(16, 256), weight, weight, weight, weight],
     )(scaled, squares, low[1], high[1], low[2], high[2])
+    down, _ = lax.optimization_barrier((down, left_high))
+    down = in_core_order(*down, 1)
     came_left_high = shift(right_high, 1)
     came_right_low = shift(left_low, -1)
     came_left_low = shift((right_low + from_left.astype(F32)).astype(BF16), 1)
@@ -233,13 +231,14 @@
         3_600_000,
         [full(640, 1024), weight, weight],
     )(scaled, low[0], high[0])[0]
-    return kernel_call(
+    hidden = kernel_call(
         hidden_kernel,
         [((2, 640, 128), BF16)],
         10_000_000,
         3_500_000,
         [full(640, 512), full(16, 256)] + [full(656, 256)] * 3 + [full(640, 256)],
     )(own, squares, came_left_low, came_left_high, came_right_low, came_right_high)[0]
+    return hidden, down
 
 
 def near_output_kernel(own, left, right, own_down, left_down, right_down, total):
@@ -309,10 +308,10 @@
     first = lax.axis_index("core") == 0
     low = [jnp.where(first, pieces[k], swapped[k]) for k in range(4)]
     high = [jnp.where(first, swapped[k], pieces[k]) for k in range(4)]
-    down = in_core_order(down_weight[0], swap_cores(down_weight[0]), 1)
+    down = (down_weight[0], swap_cores(down_weight[0]))
     arrived = lax.all_to_all(outgoing, CTX, split_axis=0, concat_axis=0, tiled=True)
     gain = lax.dynamic_slice_in_dim(norm_gain, row * 1024, 1024)
-    hidden = expert_hidden(arrived, gain, low, high)
+    hidden, down = expert_hidden(arrived, gain, low, high, down)
     expert_out = expert_outputs(hidden, down)
     returned = lax.all_to_all(expert_out, CTX, split_axis=0, concat_axis=0, tiled=True)
     returned = returned.reshape(64 * HALF, 1024)

time: 313 us -> 312 us (level)
  transfers between devices with their start and end apart: 23 -> 23, of which waited for: 12 -> 11; matrix products, arithmetic and copies ran while one was open for 8% -> 8% of each run, Pallas kernels for 2% -> 2%
where the time goes in v4:
time: 312 us; the launch traced here: 310 us
  starting transfers between devices  118 us (38%)
  waiting for transfers between devices  99.5 us (32%)
  blocking collectives  34.2 us (11%)
  other arithmetic  14.6 us (5%)
  between operations  14.2 us (5%)
  local copies, waits for them, and re-layouts  12.3 us (4%)
  matrix products  9.5 us (3%)
  Pallas kernels  7.47 us (2%)
    ppermute x13, starting transfers between devices, shift(): return lax.ppermute(block, 'y_hi', [(i, (i + step) % 4) for i in range(4)])  52.5 us
    all_to_all x1, waiting for transfers between devices, per_device(): lax.all_to_all(expert_out, CTX, split_axis=0, concat_axis=0, tiled=True)  34 us
    ppermute x13, waiting for transfers between devices, shift(): return lax.ppermute(block, 'y_hi', [(i, (i + step) % 4) for i in range(4)])  31.9 us
    all_to_all x1, starting transfers between devices, per_device(): lax.all_to_all(expert_out, CTX, split_axis=0, concat_axis=0, tiled=True)  19 us
    all_gather x1, blocking collectives, attention_rows(): attention = lax.all_gather(mine, EXP, axis=0, tiled=False)  17.3 us
    all_to_all x1, waiting for transfers between devices, per_device(): lax.all_to_all(outgoing, CTX, split_axis=0, concat_axis=0, tiled=True)  17.3 us
    all_gather x1, blocking collectives, attention_rows(): lax.all_gather(jnp.concatenate([queries, out_weight.T], axis=0), EXP, axi...  16.9 us
    all_to_all x1, starting transfers between devices, attention_rows(): held = lax.all_to_all(spread, CTX, split_axis=0, concat_axis=0, tiled=True)  15.3 us
  transfers between devices with their start and end apart: 23, of which 11 were waited for; matrix products, arithmetic and copies ran while one was open for 8% of the time, Pallas kernels for 2%

profile of v4, /device:TPU:1, one launch (start us, length us, event | category | flops | bytes accessed | tf_op | source)
XLA Modules:
  0.0 310.2 jit_solution(10412107486853654549)
XLA Ops:
  8.2 15.3 %all-to-all-start = ((bf16[64,16,256]{2,1,0:T(8,128)(2,1)}), bf16[64,16,256]{2,1,0:T(8,128)(2,1)S(1)}, u32[]{:S(2)}, u32[]{:S(2)}) async-start(bf16[64,16,256]{2,1,0:T(8,128)(2,1)} %broadcast_in_dim.83), calls=%async_computation | async-start | bytes 1048576 | tf_op jit(solution)/shard_map/all_to_all | solution.py:73
  24.4 2.7 fusion.17
  27.2 16.9 %all-gather = bf16[1536,128]{1,0:T(8,128)(2,1)S(1)} all-gather(bf16[192,128]{1,0:T(8,128)(2,1)S(1)} %pad_maximum_fusion.1), channel_id=2, replica_groups=mesh['y_lo'=2,'x'=4,'z'=8,'y_hi'=4,'core'=2] {'y_hi','core'}, dimensions={0}, use_global_device_ids=true | all-gather | bytes 442368 | tf_op jit(solution)/shard_map/all_gather | solution.py:63
  44.1 3.3 %collective-permute-start.2 = (bf16[8,64,128]{2,1,0:T(8,128)(2,1)S(1)}, bf16[8,64,128]{2,1,0:T(8,128)(2,1)S(1)}, u32[]{:S(2)}, u32[]{:S(2)}) collective-permute-start(bf16[8,64,128]{2,1,0:T(8,128)(2,1)S(1)} %slice.109), channel_id=1, source_target_pairs={{0,0},{1,64},{2,128},{3,192},{4,256},{5,320},{6,384},{7,448},{64,1... | collective-permute-start | bytes 393224 | tf_op jit(solution)/shard_map/ppermute | solution.py:34
  47.3 5.2 %collective-permute-start = (bf16[1024,256]{1,0:T(8,128)(2,1)}, bf16[1024,256]{1,0:T(8,128)(2,1)S(1)}, u32[]{:S(2)}, u32[]{:S(2)}) collective-permute-start(bf16[1024,256]{1,0:T(8,128)(2,1)} %get-tuple-element.26), channel_id=1, source_target_pairs={{0,2},{2,4},{4,6},{6,0},{1,3},{3,5},{5,7},{7,1},{8,10},{10,12},{12... | collective-permute-start | bytes 1572872 | tf_op jit(solution)/shard_map/ppermute | solution.py:42
  52.6 4.5 %collective-permute-start.1 = (bf16[1024,256]{1,0:T(8,128)(2,1)}, bf16[1024,256]{1,0:T(8,128)(2,1)S(1)}, u32[]{:S(2)}, u32[]{:S(2)}) collective-permute-start(bf16[1024,256]{1,0:T(8,128)(2,1)} %get-tuple-element.27), channel_id=1, source_target_pairs={{0,6},{2,0},{4,2},{6,4},{1,7},{3,1},{5,3},{7,5},{8,14},{10,8},{12,... | collective-permute-start | bytes 1572872 | tf_op jit(solution)/shard_map/ppermute | solution.py:42
  63.8 5.1 %all-to-all-start.1 = ((bf16[8,144,128]{2,1,0:T(8,128)(2,1)}), bf16[8,144,128]{2,1,0:T(8,128)(2,1)S(1)}, u32[]{:S(2)}, u32[]{:S(2)}) async-start(bf16[8,144,128]{2,1,0:T(8,128)(2,1)} %concatenate.36), calls=%async_computation.1 | async-start | bytes 589824 | tf_op jit(solution)/shard_map/all_to_all | solution.py:93
  69.5 14.7 %all-to-all-done.1 = bf16[8,144,128]{2,1,0:T(8,128)(2,1)S(1)} async-done(((bf16[8,144,128]{2,1,0:T(8,128)(2,1)}), bf16[8,144,128]{2,1,0:T(8,128)(2,1)S(1)}, u32[]{:S(2)}, u32[]{:S(2)}) %all-to-all-start.1) | async-done | bytes 294944 | tf_op jit(solution)/shard_map/all_to_all | solution.py:93
  84.5 17.3 %all-gather.1 = bf16[1024,128]{1,0:T(8,128)(2,1)S(1)} all-gather(bf16[128,128]{1,0:T(8,128)(2,1)S(1)} %multiply_reduce_fusion), channel_id=3, replica_groups=mesh['y_lo'=2,'x'=4,'z'=8,'y_hi'=4,'core'=2] {'y_hi','core'}, dimensions={0}, use_global_device_ids=true | all-gather | bytes 294912 | tf_op jit(solution)/shard_map/all_gather | solution.py:101
  105.8 6.8 %collective-permute-start.4 = (bf16[1024,256]{1,0:T(8,128)(2,1)}, bf16[1024,256]{1,0:T(8,128)(2,1)}, u32[]{:S(2)}, u32[]{:S(2)}) collective-permute-start(bf16[1024,256]{1,0:T(8,128)(2,1)} %get-tuple-element.32), channel_id=1, source_target_pairs={{0,4},{2,6},{4,0},{6,2},{1,5},{3,7},{5,1},{7,3},{8,12},{10,14},{12... | collective-permute-start | bytes 1572872 | tf_op jit(solution)/shard_map/ppermute | solution.py:42
  116.0 10.5 %all-to-all-start.2 = ((bf16[64,80,128]{2,1,0:T(8,128)(2,1)}), bf16[64,80,128]{2,1,0:T(8,128)(2,1)}, u32[]{:S(2)}, u32[]{:S(2)}) async-start(bf16[64,80,128]{2,1,0:T(8,128)(2,1)} %reshape.209), calls=%async_computation.2 | async-start | bytes 2621440 | tf_op jit(solution)/shard_map/all_to_all | solution.py:312
  126.6 4.5 %collective-permute-done.4 = bf16[1024,256]{1,0:T(8,128)(2,1)} collective-permute-done((bf16[1024,256]{1,0:T(8,128)(2,1)}, bf16[1024,256]{1,0:T(8,128)(2,1)}, u32[]{:S(2)}, u32[]{:S(2)}) %collective-permute-start.4) | collective-permute-done | bytes 524320 | tf_op jit(solution)/shard_map/ppermute | solution.py:42
  132.5 3.9 %collective-permute-start.5 = (bf16[4,1024,256]{2,1,0:T(8,128)(2,1)S(1)}, bf16[4,1024,256]{2,1,0:T(8,128)(2,1)}, u32[]{:S(2)}, u32[]{:S(2)}) collective-permute-start(bf16[4,1024,256]{2,1,0:T(8,128)(2,1)S(1)} %pad_maximum_fusion), channel_id=1, source_target_pairs={{0,1},{1,0},{2,3},{3,2},{4,5},{5,4},{6,7},{7,6},{8,9},{9,8},{10,11... | collective-permute-start | bytes 6291464 | tf_op jit(solution)/shard_map/ppermute | solution.py:38
  140.2 2.9 broadcast_select_fusion.2
  143.1 17.3 %all-to-all-done.2 = bf16[64,80,128]{2,1,0:T(8,128)(2,1)} async-done(((bf16[64,80,128]{2,1,0:T(8,128)(2,1)}), bf16[64,80,128]{2,1,0:T(8,128)(2,1)}, u32[]{:S(2)}, u32[]{:S(2)}) %all-to-all-start.2) | async-done | bytes 1310752 | tf_op jit(solution)/shard_map/all_to_all | solution.py:312
  160.4 4.5 %shard_map.100 = (bf16[640,1024]{1,0:T(8,128)(2,1)}, bf16[16,256]{1,0:T(8,128)(2,1)}, bf16[656,256]{1,0:T(8,128)(2,1)}, bf16[640,256]{1,0:T(8,128)(2,1)}) custom-call(bf16[5120,128]{1,0:T(8,128)(2,1)} %bitcast.22.arrived, f32[1,1024]{1,0:T(1,128)} %bitcast.118, bf16[1024,256]{1,0:T(8,128)(2,1)} %get-tuple-element.63.low_weight, ...), custom_call_target="tpu_custom_call" | custom-call | flops 680000000 | bytes 4500000 | tf_op jit(solution)/shard_map/pallas_call | solution.py:204
  164.9 2.5 collective-permute-start.10
  168.5 3.7 %collective-permute-start.6 = (bf16[656,256]{1,0:T(8,128)(2,1)}, bf16[656,256]{1,0:T(8,128)(2,1)S(1)}, u32[]{:S(2)}, u32[]{:S(2)}) collective-permute-start(bf16[656,256]{1,0:T(8,128)(2,1)} %get-tuple-element.38), channel_id=1, source_target_pairs={{0,2},{2,4},{4,6},{6,0},{1,3},{3,5},{5,7},{7,1},{8,10},{10,12},{12... | collective-permute-start | bytes 1007624 | tf_op jit(solution)/shard_map/ppermute | solution.py:42
  175.8 2.9 collective-permute-start.8
  178.7 4.5 %collective-permute-start.9 = (bf16[656,256]{1,0:T(8,128)(2,1)S(1)}, bf16[656,256]{1,0:T(8,128)(2,1)S(1)}, u32[]{:S(2)}, u32[]{:S(2)}) collective-permute-start(bf16[656,256]{1,0:T(8,128)(2,1)S(1)} %get-tuple-element.40), channel_id=1, source_target_pairs={{0,6},{2,0},{4,2},{6,4},{1,7},{3,1},{5,3},{7,5},{8,14},{10,8},{12,... | collective-permute-start | bytes 1007624 | tf_op jit(solution)/shard_map/ppermute | solution.py:42
  183.3 2.5 collective-permute-start.11
  185.9 3.7 %collective-permute-start.7 = (bf16[656,256]{1,0:T(8,128)(2,1)S(1)}, bf16[656,256]{1,0:T(8,128)(2,1)S(1)}, u32[]{:S(2)}, u32[]{:S(2)}) collective-permute-start(bf16[656,256]{1,0:T(8,128)(2,1)S(1)} %add_convert_fusion.1), channel_id=1, source_target_pairs={{0,2},{2,4},{4,6},{6,0},{1,3},{3,5},{5,7},{7,1},{8,10},{10,12},{12... | collective-permute-start | bytes 1007624 | tf_op jit(solution)/shard_map/ppermute | solution.py:42
  192.4 11.0 %collective-permute-done.11.right_high = bf16[640,256]{1,0:T(8,128)(2,1)S(1)} collective-permute-done((bf16[640,256]{1,0:T(8,128)(2,1)S(1)}, bf16[640,256]{1,0:T(8,128)(2,1)S(1)}, u32[]{:S(2)}, u32[]{:S(2)}) %collective-permute-start.11) | collective-permute-done | bytes 327712 | tf_op jit(solution)/shard_map/ppermute | solution.py:42
  204.0 5.7 %collective-permute-start.14 = (bf16[2,640,128]{2,1,0:T(8,128)(2,1)S(1)}, bf16[2,640,128]{2,1,0:T(8,128)(2,1)S(1)}, u32[]{:S(2)}, u32[]{:S(2)}) collective-permute-start(bf16[2,640,128]{2,1,0:T(8,128)(2,1)S(1)} %shard_map.103), channel_id=1, source_target_pairs={{0,6},{2,0},{4,2},{6,4},{1,7},{3,1},{5,3},{7,5},{8,14},{10,8},{12,... | collective-permute-start | bytes 983048 | tf_op jit(solution)/shard_map/ppermute | solution.py:42
  212.6 4.9 %collective-permute-done.14 = bf16[2,640,128]{2,1,0:T(8,128)(2,1)S(1)} collective-permute-done((bf16[2,640,128]{2,1,0:T(8,128)(2,1)S(1)}, bf16[2,640,128]{2,1,0:T(8,128)(2,1)S(1)}, u32[]{:S(2)}, u32[]{:S(2)}) %collective-permute-start.14) | collective-permute-done | bytes 327712 | tf_op jit(solution)/shard_map/ppermute | solution.py:42
  217.5 5.2 %collective-permute-start.16 = (bf16[640,128]{1,0:T(8,128)(2,1)S(1)}, bf16[640,128]{1,0:T(8,128)(2,1)S(1)}, u32[]{:S(2)}, u32[]{:S(2)}) collective-permute-start(bf16[640,128]{1,0:T(8,128)(2,1)S(1)} %slice_bitcast_fusion.3), channel_id=1, source_target_pairs={{0,6},{2,0},{4,2},{6,4},{1,7},{3,1},{5,3},{7,5},{8,14},{10,8},{12,... | collective-permute-start | bytes 491528 | tf_op jit(solution)/shard_map/ppermute | solution.py:42
  222.9 3.4 %collective-permute-start.15 = (bf16[640,128]{1,0:T(8,128)(2,1)S(1)}, bf16[640,128]{1,0:T(8,128)(2,1)S(1)}, u32[]{:S(2)}, u32[]{:S(2)}) collective-permute-start(bf16[640,128]{1,0:T(8,128)(2,1)S(1)} %slice_bitcast_fusion.8), channel_id=1, source_target_pairs={{0,2},{2,4},{4,6},{6,0},{1,3},{3,5},{5,7},{7,1},{8,10},{10,12},{12... | collective-permute-start | bytes 491528 | tf_op jit(solution)/shard_map/ppermute | solution.py:42
  228.2 6.9 %collective-permute-done.16 = bf16[640,128]{1,0:T(8,128)(2,1)S(1)} collective-permute-done((bf16[640,128]{1,0:T(8,128)(2,1)S(1)}, bf16[640,128]{1,0:T(8,128)(2,1)S(1)}, u32[]{:S(2)}, u32[]{:S(2)}) %collective-permute-start.16) | collective-permute-done | bytes 163872 | tf_op jit(solution)/shard_map/ppermute | solution.py:42
  235.6 4.4 %collective-permute-done.15 = bf16[640,128]{1,0:T(8,128)(2,1)S(1)} collective-permute-done((bf16[640,128]{1,0:T(8,128)(2,1)S(1)}, bf16[640,128]{1,0:T(8,128)(2,1)S(1)}, u32[]{:S(2)}, u32[]{:S(2)}) %collective-permute-start.15) | collective-permute-done | bytes 163872 | tf_op jit(solution)/shard_map/ppermute | solution.py:42
  242.6 19.0 %all-to-all-start.3 = ((bf16[64,80,128]{2,1,0:T(8,128)(2,1)}), bf16[64,80,128]{2,1,0:T(8,128)(2,1)S(1)}, u32[]{:S(2)}, u32[]{:S(2)}) async-start(bf16[64,80,128]{2,1,0:T(8,128)(2,1)} %reshape.211), calls=%async_computation.3 | async-start | bytes 2621440 | tf_op jit(solution)/shard_map/all_to_all | solution.py:316
  261.6 34.0 %all-to-all-done.3 = bf16[64,80,128]{2,1,0:T(8,128)(2,1)S(1)} async-done(((bf16[64,80,128]{2,1,0:T(8,128)(2,1)}), bf16[64,80,128]{2,1,0:T(8,128)(2,1)S(1)}, u32[]{:S(2)}, u32[]{:S(2)}) %all-to-all-start.3) | async-done | bytes 1310752 | tf_op jit(solution)/shard_map/all_to_all | solution.py:316
  297.0 4.5 %collective-permute-start.17 = (f32[128,512]{1,0:T(8,128)S(1)}, f32[128,512]{1,0:T(8,128)S(1)}, u32[]{:S(2)}, u32[]{:S(2)}) collective-permute-start(f32[128,512]{1,0:T(8,128)S(1)} %slice_select_fusion), channel_id=1, source_target_pairs={{0,1},{1,0},{2,3},{3,2},{4,5},{5,4},{6,7},{7,6},{8,9},{9,8},{10,11... | collective-permute-start | bytes 786440 | tf_op jit(solution)/shard_map/ppermute | solution.py:38
  (119 shorter events, 41.8 us)
Async XLA Ops:
  8.2 49.8 %all-to-all-start = ((bf16[64,16,256]{2,1,0:T(8,128)(2,1)}), bf16[64,16,256]{2,1,0:T(8,128)(2,1)S(1)}, u32[]{:S(2)}, u32[]{:S(2)}) async-start(bf16[64,16,256]{2,1,0:T(8,128)(2,1)} %broadcast_in_dim.83), calls=%async_computation | async-start | bytes 1048576 | tf_op jit(solution)/shard_map/all_to_all | solution.py:73
  23.6 78.3 %all-gather.5.cloned.1.call-start = ((), (), s32[]{:S(2)}) async-start(), calls=%async_computation.4 | async-start | bytes 1179648 | tf_op jit(solution)/shard_map/all_gather | solution.py:70
  44.1 13.2 %collective-permute-start.2 = (bf16[8,64,128]{2,1,0:T(8,128)(2,1)S(1)}, bf16[8,64,128]{2,1,0:T(8,128)(2,1)S(1)}, u32[]{:S(2)}, u32[]{:S(2)}) collective-permute-start(bf16[8,64,128]{2,1,0:T(8,128)(2,1)S(1)} %slice.109), channel_id=1, source_target_pairs={{0,0},{1,64},{2,128},{3,192},{4,256},{5,320},{6,384},{7,448},{64,1... | collective-permute-start | bytes 393224 | tf_op jit(solution)/shard_map/ppermute | solution.py:34
  47.3 37.2 %collective-permute-start = (bf16[1024,256]{1,0:T(8,128)(2,1)}, bf16[1024,256]{1,0:T(8,128)(2,1)S(1)}, u32[]{:S(2)}, u32[]{:S(2)}) collective-permute-start(bf16[1024,256]{1,0:T(8,128)(2,1)} %get-tuple-element.26), channel_id=1, source_target_pairs={{0,2},{2,4},{4,6},{6,0},{1,3},{3,5},{5,7},{7,1},{8,10},{10,12},{12... | collective-permute-start | bytes 1572872 | tf_op jit(solution)/shard_map/ppermute | solution.py:42
  52.6 31.9 %collective-permute-start.1 = (bf16[1024,256]{1,0:T(8,128)(2,1)}, bf16[1024,256]{1,0:T(8,128)(2,1)S(1)}, u32[]{:S(2)}, u32[]{:S(2)}) collective-permute-start(bf16[1024,256]{1,0:T(8,128)(2,1)} %get-tuple-element.27), channel_id=1, source_target_pairs={{0,6},{2,0},{4,2},{6,4},{1,7},{3,1},{5,3},{7,5},{8,14},{10,8},{12,... | collective-permute-start | bytes 1572872 | tf_op jit(solution)/shard_map/ppermute | solution.py:42
  60.4 8.7 %copy-start.13 = (s32[128,8]{0,1:T(8,128)S(1)}, s32[128,8]{0,1:T(8,128)}, u32[]{:S(2)}) copy-start(s32[128,8]{0,1:T(8,128)} %param.15) | copy-start | bytes 12292
  60.4 8.7 %copy-start.14 = (f32[128,8]{0,1:T(8,128)S(1)}, f32[128,8]{0,1:T(8,128)}, u32[]{:S(2)}) copy-start(f32[128,8]{0,1:T(8,128)} %param.16) | copy-start | bytes 12292
  63.8 20.4 %all-to-all-start.1 = ((bf16[8,144,128]{2,1,0:T(8,128)(2,1)}), bf16[8,144,128]{2,1,0:T(8,128)(2,1)S(1)}, u32[]{:S(2)}, u32[]{:S(2)}) async-start(bf16[8,144,128]{2,1,0:T(8,128)(2,1)} %concatenate.36), calls=%async_computation.1 | async-start | bytes 589824 | tf_op jit(solution)/shard_map/all_to_all | solution.py:93
  69.2 34.5 %copy-start.12 = (bf16[128,512]{1,0:T(8,128)(2,1)S(1)}, bf16[128,512]{1,0:T(8,128)(2,1)}, u32[]{:S(2)}) copy-start(bf16[128,512]{1,0:T(8,128)(2,1)} %param.10) | copy-start | bytes 393220
  84.5 30.0 %copy-start.5 = (bf16[1024,256]{1,0:T(8,128)(2,1)}, bf16[1024,256]{1,0:T(8,128)(2,1)S(1)}, u32[]{:S(2)}) copy-start(bf16[1024,256]{1,0:T(8,128)(2,1)S(1)} %collective-permute-done.1) | copy-start | bytes 1572868
  103.7 9.8 %copy-start.6 = (bf16[128,512]{1,0:T(8,128)(2,1)}, bf16[128,512]{1,0:T(8,128)(2,1)S(1)}, u32[]{:S(2)}) copy-start(bf16[128,512]{1,0:T(8,128)(2,1)S(1)} %add_convert_fusion.4) | copy-start | bytes 393220
  103.7 9.8 %collective-permute-start.3 = (bf16[128,512]{1,0:T(8,128)(2,1)S(1)}, bf16[128,512]{1,0:T(8,128)(2,1)S(1)}, u32[]{:S(2)}, u32[]{:S(2)}) collective-permute-start(bf16[128,512]{1,0:T(8,128)(2,1)S(1)} %add_convert_fusion.4), channel_id=1, source_target_pairs={{0,1},{1,0},{2,3},{3,2},{4,5},{5,4},{6,7},{7,6},{8,9},{9,8},{10,11... | collective-permute-start | bytes 393224 | tf_op jit(solution)/shard_map/ppermute | solution.py:38
  105.8 25.2 %collective-permute-start.4 = (bf16[1024,256]{1,0:T(8,128)(2,1)}, bf16[1024,256]{1,0:T(8,128)(2,1)}, u32[]{:S(2)}, u32[]{:S(2)}) collective-permute-start(bf16[1024,256]{1,0:T(8,128)(2,1)} %get-tuple-element.32), channel_id=1, source_target_pairs={{0,4},{2,6},{4,0},{6,2},{1,5},{3,7},{5,1},{7,3},{8,12},{10,14},{12... | collective-permute-start | bytes 1572872 | tf_op jit(solution)/shard_map/ppermute | solution.py:42
  116.0 44.3 %all-to-all-start.2 = ((bf16[64,80,128]{2,1,0:T(8,128)(2,1)}), bf16[64,80,128]{2,1,0:T(8,128)(2,1)}, u32[]{:S(2)}, u32[]{:S(2)}) async-start(bf16[64,80,128]{2,1,0:T(8,128)(2,1)} %reshape.209), calls=%async_computation.2 | async-start | bytes 2621440 | tf_op jit(solution)/shard_map/all_to_all | solution.py:312
  132.5 7.8 %collective-permute-start.5 = (bf16[4,1024,256]{2,1,0:T(8,128)(2,1)S(1)}, bf16[4,1024,256]{2,1,0:T(8,128)(2,1)}, u32[]{:S(2)}, u32[]{:S(2)}) collective-permute-start(bf16[4,1024,256]{2,1,0:T(8,128)(2,1)S(1)} %pad_maximum_fusion), channel_id=1, source_target_pairs={{0,1},{1,0},{2,3},{3,2},{4,5},{5,4},{6,7},{7,6},{8,9},{9,8},{10,11... | collective-permute-start | bytes 6291464 | tf_op jit(solution)/shard_map/ppermute | solution.py:38
  136.3 39.4 %collective-permute-start.12 = (bf16[1024,512]{1,0:T(8,128)(2,1)}, bf16[1024,512]{1,0:T(8,128)(2,1)}, u32[]{:S(2)}, u32[]{:S(2)}) collective-permute-start(bf16[1024,512]{1,0:T(8,128)(2,1)} %bitcast.33), channel_id=1, source_target_pairs={{0,1},{1,0},{2,3},{3,2},{4,5},{5,4},{6,7},{7,6},{8,9},{9,8},{10,11... | collective-permute-start | bytes 3145736 | tf_op jit(solution)/shard_map/ppermute | solution.py:38
  164.9 18.3 %collective-permute-start.10 = (bf16[640,256]{1,0:T(8,128)(2,1)}, bf16[640,256]{1,0:T(8,128)(2,1)S(1)}, u32[]{:S(2)}, u32[]{:S(2)}) collective-permute-start(bf16[640,256]{1,0:T(8,128)(2,1)} %get-tuple-element.42), channel_id=1, source_target_pairs={{0,6},{2,0},{4,2},{6,4},{1,7},{3,1},{5,3},{7,5},{8,14},{10,8},{12,... | collective-permute-start | bytes 983048 | tf_op jit(solution)/shard_map/ppermute | solution.py:42
  168.5 17.3 %collective-permute-start.6 = (bf16[656,256]{1,0:T(8,128)(2,1)}, bf16[656,256]{1,0:T(8,128)(2,1)S(1)}, u32[]{:S(2)}, u32[]{:S(2)}) collective-permute-start(bf16[656,256]{1,0:T(8,128)(2,1)} %get-tuple-element.38), channel_id=1, source_target_pairs={{0,2},{2,4},{4,6},{6,0},{1,3},{3,5},{5,7},{7,1},{8,10},{10,12},{12... | collective-permute-start | bytes 1007624 | tf_op jit(solution)/shard_map/ppermute | solution.py:42
  175.8 16.6 %collective-permute-start.8 = (bf16[656,256]{1,0:T(8,128)(2,1)S(1)}, bf16[656,256]{1,0:T(8,128)(2,1)S(1)}, u32[]{:S(2)}, u32[]{:S(2)}) collective-permute-start(bf16[656,256]{1,0:T(8,128)(2,1)S(1)} %get-tuple-element.39), channel_id=1, source_target_pairs={{0,2},{2,4},{4,6},{6,0},{1,3},{3,5},{5,7},{7,1},{8,10},{10,12},{12... | collective-permute-start | bytes 1007624 | tf_op jit(solution)/shard_map/ppermute | solution.py:42
  178.7 13.7 %collective-permute-start.9 = (bf16[656,256]{1,0:T(8,128)(2,1)S(1)}, bf16[656,256]{1,0:T(8,128)(2,1)S(1)}, u32[]{:S(2)}, u32[]{:S(2)}) collective-permute-start(bf16[656,256]{1,0:T(8,128)(2,1)S(1)} %get-tuple-element.40), channel_id=1, source_target_pairs={{0,6},{2,0},{4,2},{6,4},{1,7},{3,1},{5,3},{7,5},{8,14},{10,8},{12,... | collective-permute-start | bytes 1007624 | tf_op jit(solution)/shard_map/ppermute | solution.py:42
  183.3 20.1 %collective-permute-start.11 = (bf16[640,256]{1,0:T(8,128)(2,1)S(1)}, bf16[640,256]{1,0:T(8,128)(2,1)S(1)}, u32[]{:S(2)}, u32[]{:S(2)}) collective-permute-start(bf16[640,256]{1,0:T(8,128)(2,1)S(1)} %add_convert_fusion.2), channel_id=1, source_target_pairs={{0,6},{2,0},{4,2},{6,4},{1,7},{3,1},{5,3},{7,5},{8,14},{10,8},{12,... | collective-permute-start | bytes 983048 | tf_op jit(solution)/shard_map/ppermute | solution.py:42
  185.9 17.5 %collective-permute-start.7 = (bf16[656,256]{1,0:T(8,128)(2,1)S(1)}, bf16[656,256]{1,0:T(8,128)(2,1)S(1)}, u32[]{:S(2)}, u32[]{:S(2)}) collective-permute-start(bf16[656,256]{1,0:T(8,128)(2,1)S(1)} %add_convert_fusion.1), channel_id=1, source_target_pairs={{0,2},{2,4},{4,6},{6,0},{1,3},{3,5},{5,7},{7,1},{8,10},{10,12},{12... | collective-permute-start | bytes 1007624 | tf_op jit(solution)/shard_map/ppermute | solution.py:42
  192.1 11.3 %copy-start.4 = (bf16[16,256]{1,0:T(8,128)(2,1)S(1)}, bf16[16,256]{1,0:T(8,128)(2,1)}, u32[]{:S(2)}) copy-start(bf16[16,256]{1,0:T(8,128)(2,1)} %get-tuple-element.36.squares) | copy-start | bytes 24580
  204.0 13.5 %collective-permute-start.14 = (bf16[2,640,128]{2,1,0:T(8,128)(2,1)S(1)}, bf16[2,640,128]{2,1,0:T(8,128)(2,1)S(1)}, u32[]{:S(2)}, u32[]{:S(2)}) collective-permute-start(bf16[2,640,128]{2,1,0:T(8,128)(2,1)S(1)} %shard_map.103), channel_id=1, source_target_pairs={{0,6},{2,0},{4,2},{6,4},{1,7},{3,1},{5,3},{7,5},{8,14},{10,8},{12,... | collective-permute-start | bytes 983048 | tf_op jit(solution)/shard_map/ppermute | solution.py:42
  209.7 13.2 %collective-permute-start.13 = (bf16[2,640,128]{2,1,0:T(8,128)(2,1)S(1)}, bf16[2,640,128]{2,1,0:T(8,128)(2,1)S(1)}, u32[]{:S(2)}, u32[]{:S(2)}) collective-permute-start(bf16[2,640,128]{2,1,0:T(8,128)(2,1)S(1)} %shard_map.103), channel_id=1, source_target_pairs={{0,2},{2,4},{4,6},{6,0},{1,3},{3,5},{5,7},{7,1},{8,10},{10,12},{12... | collective-permute-start | bytes 983048 | tf_op jit(solution)/shard_map/ppermute | solution.py:42
  217.5 17.7 %collective-permute-start.16 = (bf16[640,128]{1,0:T(8,128)(2,1)S(1)}, bf16[640,128]{1,0:T(8,128)(2,1)S(1)}, u32[]{:S(2)}, u32[]{:S(2)}) collective-permute-start(bf16[640,128]{1,0:T(8,128)(2,1)S(1)} %slice_bitcast_fusion.3), channel_id=1, source_target_pairs={{0,6},{2,0},{4,2},{6,4},{1,7},{3,1},{5,3},{7,5},{8,14},{10,8},{12,... | collective-permute-start | bytes 491528 | tf_op jit(solution)/shard_map/ppermute | solution.py:42
  222.9 17.2 %collective-permute-start.15 = (bf16[640,128]{1,0:T(8,128)(2,1)S(1)}, bf16[640,128]{1,0:T(8,128)(2,1)S(1)}, u32[]{:S(2)}, u32[]{:S(2)}) collective-permute-start(bf16[640,128]{1,0:T(8,128)(2,1)S(1)} %slice_bitcast_fusion.8), channel_id=1, source_target_pairs={{0,2},{2,4},{4,6},{6,0},{1,3},{3,5},{5,7},{7,1},{8,10},{10,12},{12... | collective-permute-start | bytes 491528 | tf_op jit(solution)/shard_map/ppermute | solution.py:42
  241.1 20.5 %copy-start.9 = (pred[640,128]{1,0:T(32,128)(4,1)S(1)}, pred[640,128]{1,0:T(32,128)(4,1)}, u32[]{:S(2)}) copy-start(pred[640,128]{1,0:T(32,128)(4,1)} %copy-done.8) | copy-start | bytes 245764
  242.6 53.7 %copy-start.10 = (bf16[640,128]{1,0:T(8,128)(2,1)S(1)}, bf16[640,128]{1,0:T(8,128)(2,1)}, u32[]{:S(2)}) copy-start(bf16[640,128]{1,0:T(8,128)(2,1)} %get-tuple-element.45) | copy-start | bytes 491524
  242.6 53.1 %all-to-all-start.3 = ((bf16[64,80,128]{2,1,0:T(8,128)(2,1)}), bf16[64,80,128]{2,1,0:T(8,128)(2,1)S(1)}, u32[]{:S(2)}, u32[]{:S(2)}) async-start(bf16[64,80,128]{2,1,0:T(8,128)(2,1)} %reshape.211), calls=%async_computation.3 | async-start | bytes 2621440 | tf_op jit(solution)/shard_map/all_to_all | solution.py:316
  296.2 7.1 %copy-start.1 = (bf16[128,256]{1,0:T(8,128)(2,1)S(1)}, bf16[128,256]{1,0:T(8,128)(2,1)}, u32[]{:S(2)}) copy-start(bf16[128,256]{1,0:T(8,128)(2,1)} %param.12) | copy-start | bytes 196612
  297.0 5.7 %collective-permute-start.17 = (f32[128,512]{1,0:T(8,128)S(1)}, f32[128,512]{1,0:T(8,128)S(1)}, u32[]{:S(2)}, u32[]{:S(2)}) collective-permute-start(f32[128,512]{1,0:T(8,128)S(1)} %slice_select_fusion), channel_id=1, source_target_pairs={{0,1},{1,0},{2,3},{3,2},{4,5},{5,4},{6,7},{7,6},{8,9},{9,8},{10,11... | collective-permute-start | bytes 786440 | tf_op jit(solution)/shard_map/ppermute | solution.py:38
  (6 other events, 10.5 us)
Sparse Core Ops, SparseCore 0:
  58.1 38.6 all-gather.4
